TPU v7x, 32 devices: a whole 2x2x4 slice. The times are simulated.
32 devices in a mesh: task: 4 (over y, x), dp: 8 (over z, core).
Axes of the slice: x: 2, y: 2, z: 4, core: 2. Of those that a mesh axis runs over, the one named last changes fastest.
Arguments:
- images: bfloat16 [64, 16, 18, 2048], P(('task', 'dp')), may hold values from -6 to 6
- sizes: int32 [64, 2], P(('task', 'dp')), may hold values from 5 to 18, as said below
- thresholds: bfloat16 [64, 16, 18, 2048], P(('task', 'dp')), may hold values from 0 to 1
- head_grad: bfloat16 [64, 16, 18, 768], P(('task', 'dp')), may hold values from -6 to 6
- w_reduce: bfloat16 [2048, 512], replicated, may hold values from -0.125 to 0.125
- w_spatial: bfloat16 [3, 3, 512, 512], replicated, may hold values from -0.09375 to 0.09375
- w_expand: bfloat16 [512, 2048], replicated, may hold values from -0.25 to 0.25
- w_heads: bfloat16 [2048, 768], replicated, may hold values from -0.125 to 0.125
- gain_a: float32 [512], replicated, may hold values from 0.5 to 1.5
- shift_a: float32 [512], replicated, may hold values from -2 to 2
- gain_b: float32 [512], replicated, may hold values from 0.5 to 1.5
- shift_b: float32 [512], replicated, may hold values from -2 to 2
- gain_c: float32 [2048], replicated, may hold values from 0.5 to 1.5
- shift_c: float32 [2048], replicated, may hold values from -2 to 2
Outputs:
- head_out: bfloat16 [64, 16, 18, 768], P(('task', 'dp'))
- grad_images: bfloat16 [64, 16, 18, 2048], P(('task', 'dp'))
- grad_reduce: float32 [2048, 512], replicated
- grad_spatial: float32 [3, 3, 512, 512], replicated
- grad_expand: float32 [512, 2048], replicated
- grad_heads: float32 [2048, 768], replicated
- grad_gain_a: float32 [512], replicated
- grad_shift_a: float32 [512], replicated
- grad_gain_b: float32 [512], replicated
- grad_shift_b: float32 [512], replicated
- grad_gain_c: float32 [2048], replicated
- grad_shift_c: float32 [2048], replicated
Inputs may be any that keep to these rules, and one draw needn't show every extreme that they name: `sizes`: each image's valid height is at most 16 and width at most 18; the last image is full and the first has height 16 // 3.
All inputs are finite; a program needn't handle non-finite values.
Results may differ from a plain program's by a relative error of at most 0.0095.
Values may be sent and summed in bfloat16 or wider, within the bound.
A program may use at most 192 MiB of HBM per device.

v0:
```python
import jax
import jax.numpy as jnp
from jax import lax
from jax.sharding import PartitionSpec as P

TASKS = 3


EPS = 1e-05
SOFT = 0.01
TEMP = 0.1


def grid_mask(sizes, height, span):
    row_index = jnp.arange(height, dtype=jnp.int32)[None, :, None]
    col_index = jnp.arange(span, dtype=jnp.int32)[None, None, :]
    inside = (row_index < sizes[:, 0, None, None]) & (col_index < sizes[:, 1, None, None])
    return inside.astype(jnp.float32)


def silu_slope(values):
    logistic = jax.nn.sigmoid(values)
    return logistic * (1.0 + values * (1.0 - logistic))


def norm_forward(values, valid):
    local_count = jnp.sum(valid)
    totals = lax.psum(
        (jnp.sum(values * valid, axis=0), jnp.sum(values * values * valid, axis=0), local_count),
        ("task", "dp"),
    )
    count = totals[2]
    center = totals[0] / count
    inverse = lax.rsqrt(totals[1] / count - center * center + EPS)
    return ((values - center) * inverse, inverse, count)


def norm_backward(upstream, normed, inverse, gain, count, valid):
    shift_grad, gain_grad = lax.psum(
        (jnp.sum(upstream, axis=0), jnp.sum(upstream * normed, axis=0)), ("task", "dp")
    )
    scaled = upstream * gain
    result = (
        valid * inverse * (scaled - gain * shift_grad / count - normed * gain * gain_grad / count)
    )
    return (result.astype(jnp.bfloat16), gain_grad, shift_grad)


def spatial_forward(hidden_low, kernel):
    height, span = (hidden_low.shape[1], hidden_low.shape[2])
    padded = jnp.pad(hidden_low, ((0, 0), (1, 1), (1, 1), (0, 0)))
    summed = None
    for row_tap in range(3):
        for col_tap in range(3):
            window = padded[:, row_tap : row_tap + height, col_tap : col_tap + span]
            term = jnp.einsum(
                "ihwc,cd->ihwd",
                window,
                kernel[row_tap, col_tap],
                preferred_element_type=jnp.float32,
            )
            summed = term if summed is None else summed + term
    return (padded, summed)


def spatial_backward(padded, grad_low, kernel):
    height, span = (grad_low.shape[1], grad_low.shape[2])
    grad_pad = jnp.zeros(padded.shape, jnp.float32)
    kernel_grads = []
    for row_tap in range(3):
        for col_tap in range(3):
            window = padded[:, row_tap : row_tap + height, col_tap : col_tap + span]
            grad_pad = grad_pad.at[:, row_tap : row_tap + height, col_tap : col_tap + span].add(
                jnp.einsum(
                    "ihwd,cd->ihwc",
                    grad_low,
                    kernel[row_tap, col_tap],
                    preferred_element_type=jnp.float32,
                )
            )
            kernel_grads.append(
                jnp.einsum("ihwc,ihwd->cd", window, grad_low, preferred_element_type=jnp.float32)
            )
    channels = kernel.shape[2]
    return (grad_pad[:, 1:-1, 1:-1], jnp.stack(kernel_grads).reshape(3, 3, channels, channels))


def graddrop(task_grads, limits):
    signed = jnp.sum(task_grads, axis=0)
    magnitude = jnp.sum(jnp.sqrt(task_grads * task_grads + SOFT), axis=0)
    purity = 0.5 * (1.0 + signed / magnitude)
    keep = jax.nn.sigmoid((purity - limits) / TEMP) * jax.nn.sigmoid(
        task_grads / TEMP
    ) + jax.nn.sigmoid((limits - purity) / TEMP) * jax.nn.sigmoid(-task_grads / TEMP)
    return jnp.sum(keep * task_grads, axis=0)


def body(
    images,
    sizes,
    thresholds,
    head_grad,
    w_reduce,
    w_spatial,
    w_expand,
    w_heads,
    gain_a,
    shift_a,
    gain_b,
    shift_b,
    gain_c,
    shift_c,
):
    count_img, height, span, wide = images.shape
    pixels = count_img * height * span
    middle = w_reduce.shape[1]
    head_width = w_heads.shape[1] // TASKS
    valid = grid_mask(sizes, height, span).reshape(pixels, 1)
    inputs = images.reshape(pixels, wide).astype(jnp.float32) * valid
    inputs_low = inputs.astype(jnp.bfloat16)
    first = jnp.dot(inputs_low, w_reduce, preferred_element_type=jnp.float32)
    normed_a, inverse_a, count = norm_forward(first, valid)
    pre_a = normed_a * gain_a + shift_a
    hidden_a = (jax.nn.silu(pre_a) * valid).astype(jnp.bfloat16)
    padded_a, second = spatial_forward(hidden_a.reshape(count_img, height, span, middle), w_spatial)
    normed_b, inverse_b, count_b = norm_forward(second.reshape(pixels, middle), valid)
    pre_b = normed_b * gain_b + shift_b
    hidden_b = (jax.nn.silu(pre_b) * valid).astype(jnp.bfloat16)
    third = jnp.dot(hidden_b, w_expand, preferred_element_type=jnp.float32)
    normed_c, inverse_c, count_c = norm_forward(third, valid)
    pre_c = normed_c * gain_c + shift_c + inputs
    trunk_low = (jax.nn.silu(pre_c) * valid).astype(jnp.bfloat16)
    grad_flat = head_grad.reshape(pixels, TASKS * head_width)
    head_vals = jnp.dot(trunk_low, w_heads, preferred_element_type=jnp.float32).astype(jnp.bfloat16)
    task_grads = jnp.einsum(
        "pkh,wkh->kpw",
        grad_flat.reshape(pixels, TASKS, head_width),
        w_heads.reshape(wide, TASKS, head_width),
        preferred_element_type=jnp.float32,
    ).astype(jnp.bfloat16)
    head_term = jnp.einsum("pw,pk->wk", trunk_low, grad_flat, preferred_element_type=jnp.float32)
    limits = thresholds.reshape(pixels, wide).astype(jnp.float32)
    merged = graddrop(task_grads.astype(jnp.float32), limits)
    upstream_c = merged * silu_slope(pre_c) * valid
    third_low, gain_c_grad, shift_c_grad = norm_backward(
        upstream_c, normed_c, inverse_c, gain_c, count, valid
    )
    grad_expand = jnp.einsum("pm,pw->mw", hidden_b, third_low, preferred_element_type=jnp.float32)
    back_b = jnp.einsum("pw,mw->pm", third_low, w_expand, preferred_element_type=jnp.float32)
    upstream_b = back_b * silu_slope(pre_b) * valid
    second_low, gain_b_grad, shift_b_grad = norm_backward(
        upstream_b, normed_b, inverse_b, gain_b, count, valid
    )
    back_a, grad_spatial = spatial_backward(
        padded_a, second_low.reshape(count_img, height, span, middle), w_spatial
    )
    upstream_a = back_a.reshape(pixels, middle) * silu_slope(pre_a) * valid
    first_low, gain_a_grad, shift_a_grad = norm_backward(
        upstream_a, normed_a, inverse_a, gain_a, count, valid
    )
    grad_reduce = jnp.einsum("pw,pm->wm", inputs_low, first_low, preferred_element_type=jnp.float32)
    back_inputs = jnp.einsum("pm,wm->pw", first_low, w_reduce, preferred_element_type=jnp.float32)
    grad_inputs = (
        ((back_inputs + upstream_c) * valid)
        .astype(jnp.bfloat16)
        .reshape(count_img, height, span, wide)
    )
    spatial_flat = grad_spatial.reshape(9 * middle, middle)
    summed = lax.psum((grad_reduce, spatial_flat, grad_expand, head_term), ("task", "dp"))
    head_out = head_vals.reshape(count_img, height, span, TASKS * head_width)
    return (
        head_out,
        grad_inputs,
        summed[0],
        summed[1].reshape(3, 3, middle, middle),
        summed[2],
        summed[3],
        gain_a_grad,
        shift_a_grad,
        gain_b_grad,
        shift_b_grad,
        gain_c_grad,
        shift_c_grad,
    )


def solution(mesh):
    in_specs = (
        P(("task", "dp"), None, None, None),
        P(("task", "dp"), None),
        P(("task", "dp"), None, None, None),
        P(("task", "dp"), None, None, None),
        P(),
        P(),
        P(),
        P(),
        P(),
        P(),
        P(),
        P(),
        P(),
        P(),
    )
    out_specs = (
        P(("task", "dp"), None, None, None),
        P(("task", "dp"), None, None, None),
        P(),
        P(),
        P(),
        P(),
        P(),
        P(),
        P(),
        P(),
        P(),
        P(),
    )
    return jax.shard_map(body, mesh=mesh, in_specs=in_specs, out_specs=out_specs, check_vma=False)
```

profile of v0, /device:TPU:0, one launch (start us, length us, event | category | flops | bytes accessed | tf_op | source)
XLA Modules:
  0.0 923.1 jit_solution(7179497508469010736)
XLA Ops:
  13.3 5.9 copy.49
  29.3 42.5 %all-reduce.7 = (f32[512]{0:T(512)S(1)}, f32[]{:T(128)}, f32[512]{0:T(512)S(1)}) all-reduce(f32[512]{0:T(512)S(1)} %get-tuple-element.153, f32[]{:T(128)} %fusion.92, f32[512]{0:T(512)S(1)} %get-tuple-element.152), channel_id=1, replica_groups=mesh['task'=4,'dp'=8] {'task','dp'}, use_global_device_ids=true, to_apply=%region_5.0 | all-reduce | flops 1025 | bytes 8200 | tf_op jit(solution)/shard_map/psum | solution.py:28
  105.2 7.0 multiply_reduce_fusion.4
  114.8 5.9 copy.54
  120.7 5.6 reshape.561
  126.3 40.2 %all-reduce.6 = (f32[512]{0:T(512)S(1)}, f32[512]{0:T(512)S(1)}) all-reduce(f32[512]{0:T(512)S(1)} %get-tuple-element.151, f32[512]{0:T(512)S(1)} %get-tuple-element.150), channel_id=1, replica_groups=mesh['task'=4,'dp'=8] {'task','dp'}, use_global_device_ids=true, to_apply=%region_9.10 | all-reduce | flops 1024 | bytes 8192 | tf_op jit(solution)/shard_map/psum | solution.py:28
  172.4 40.5 %all-reduce.5 = (f32[2048]{0:T(1024)S(1)}, f32[2048]{0:T(1024)S(1)}) all-reduce(f32[2048]{0:T(1024)S(1)} %get-tuple-element.147, f32[2048]{0:T(1024)S(1)} %get-tuple-element.146), channel_id=1, replica_groups=mesh['task'=4,'dp'=8] {'task','dp'}, use_global_device_ids=true, to_apply=%region_13.14 | all-reduce | flops 4096 | bytes 32768 | tf_op jit(solution)/shard_map/psum | solution.py:28
  213.6 18.2 %fusion.2 = (f32[576,2048]{1,0:T(8,128)}, f32[576,2048]{1,0:T(8,128)}, bf16[3,576,2048]{2,1,0:T(8,128)(2,1)}) fusion(bf16[2048,3,256]{0,2,1:T(8,128)(2,1)} %bitcast.193, bf16[576,3,256]{2,1,0:T(4,128)(2,1)} %reshape_reshape.6), kind=kOutput, calls=%fused_computation.7 | convolution fusion | flops 1830813696 | bytes 20545536 | tf_op jit(solution)/shard_map/pkh,wkh->kpw/dot_general | solution.py:135
  231.8 6.0 add_divide_fusion.1
  237.9 10.1 %fusion.15 = f32[576,2048]{1,0:T(8,128)S(1)} fusion(bf16[3,576,2048]{2,1,0:T(8,128)(2,1)} %get-tuple-element.203, f32[576,2048]{1,0:T(8,128)S(1)} %get-tuple-element.180, f32[576,2048]{1,0:T(8,128)S(1)} %get-tuple-element.179), kind=kLoop, calls=%fused_computation.20 | loop fusion | flops 51904512 | bytes 21233664 | tf_op jit(solution)/shard_map/reduce_sum | solution.py:95
  253.6 40.3 %all-reduce.4 = (f32[2048]{0:T(1024)S(1)}, f32[2048]{0:T(1024)S(1)}) all-reduce(f32[2048]{0:T(1024)S(1)} %get-tuple-element.149, f32[2048]{0:T(1024)S(1)} %get-tuple-element.148), channel_id=1, replica_groups=mesh['task'=4,'dp'=8] {'task','dp'}, use_global_device_ids=true, to_apply=%region_20.21 | all-reduce | flops 4096 | bytes 32768 | tf_op jit(solution)/shard_map/psum | solution.py:39
  308.1 40.1 %all-reduce.3 = (f32[512]{0:T(512)S(1)}, f32[512]{0:T(512)S(1)}) all-reduce(f32[512]{0:T(512)S(1)} %get-tuple-element.157, f32[512]{0:T(512)S(1)} %get-tuple-element.156), channel_id=1, replica_groups=mesh['task'=4,'dp'=8] {'task','dp'}, use_global_device_ids=true, to_apply=%region_24.25 | all-reduce | flops 1024 | bytes 8192 | tf_op jit(solution)/shard_map/psum | solution.py:39
  359.5 8.5 scatter-add.31
  372.9 8.4 scatter-add.34
  384.3 7.3 scatter-add.35
  394.6 7.3 scatter-add.36
  404.9 7.3 scatter-add.39
  415.2 7.2 scatter-add.40
  425.5 7.2 scatter-add.41
  435.7 7.2 scatter-add.44
  450.0 40.3 %all-reduce.2 = (f32[512]{0:T(512)S(1)}, f32[512]{0:T(512)S(1)}) all-reduce(f32[512]{0:T(512)S(1)} %get-tuple-element.155, f32[512]{0:T(512)S(1)} %get-tuple-element.154), channel_id=1, replica_groups=mesh['task'=4,'dp'=8] {'task','dp'}, use_global_device_ids=true, to_apply=%region_29.30 | all-reduce | flops 1024 | bytes 8192 | tf_op jit(solution)/shard_map/psum | solution.py:39
  521.7 6.7 multiply_convert_fusion
  537.7 359.5 %all-reduce.11.cloned.1.call-done = (f32[2048,512]{1,0:T(8,128)}, f32[3,3,512,512]{3,2,1,0:T(8,128)}, f32[512,2048]{1,0:T(8,128)}, f32[2048,768]{1,0:T(8,128)}) async-done(((f32[2048,512]{1,0:T(8,128)}, f32[3,3,512,512]{3,2,1,0:T(8,128)}, f32[512,2048]{1,0:T(8,128)}, f32[2048,768]{1,0:T(8,128)}), (f32[2048,512]{1,0:T(8,128)}, f32[3,3,512,512]{3,2,1,0:T(8,128)}, f32[512,2048]{1,0:T(8,128)}, ...) | async-done | bytes 24117264 | tf_op jit(solution)/shard_map/psum | solution.py:169
  901.9 8.7 copy.156
  (171 shorter events, 170.1 us)
Async XLA Ops:
  7.2 160.0 %copy-start = (bf16[512,2048]{1,0:T(8,128)(2,1)S(1)}, bf16[512,2048]{1,0:T(8,128)(2,1)}, u32[]{:S(2)}) copy-start(bf16[512,2048]{1,0:T(8,128)(2,1)} %param.38) | copy-start | bytes 6291460
  7.2 889.9 %all-reduce.11.cloned.1.call-start = ((), (), s32[]{:S(2)}) async-start(), calls=%async_computation | async-start | bytes 48234496 | tf_op jit(solution)/shard_map/psum | solution.py:169
  24.7 47.7 %copy-start.23 = (f32[512]{0:T(512)S(1)}, f32[512]{0:T(512)}, u32[]{:S(2)}) copy-start(f32[512]{0:T(512)} %param.40) | copy-start | bytes 6148
  24.7 47.7 %copy-start.25 = (f32[512]{0:T(512)S(1)}, f32[512]{0:T(512)}, u32[]{:S(2)}) copy-start(f32[512]{0:T(512)} %param.41) | copy-start | bytes 6148
  29.3 43.2 %copy-start.6 = (f32[576,512]{1,0:T(8,128)}, f32[576,512]{1,0:T(8,128)S(1)}, u32[]{:S(2)}) copy-start(f32[576,512]{1,0:T(8,128)S(1)} %get-tuple-element.200) | copy-start | bytes 3538948
  120.7 46.5 %copy-start.28 = (f32[512]{0:T(512)S(1)}, f32[512]{0:T(512)}, u32[]{:S(2)}) copy-start(f32[512]{0:T(512)} %param.42) | copy-start | bytes 6148
  120.7 46.5 %copy-start.33 = (f32[512]{0:T(512)S(1)}, f32[512]{0:T(512)}, u32[]{:S(2)}) copy-start(f32[512]{0:T(512)} %param.43) | copy-start | bytes 6148
  213.5 18.2 %slice-start.6 = ((s8[4718592]{0:T(1024)(128)(4,1)}), s8[4194304]{0:T(1024)(128)(4,1)S(1)}, s32[]{:S(2)}) async-start(s8[4718592]{0:T(1024)(128)(4,1)} %bitcast.188), calls=%async_computation.7 | async-start | bytes 8388608
  213.5 18.2 %slice-start.7 = ((s8[4718592]{0:T(1024)(128)(4,1)}), s8[524288]{0:T(1024)(128)(4,1)S(1)}, s32[]{:S(2)}) async-start(s8[4718592]{0:T(1024)(128)(4,1)} %bitcast.188), calls=%async_computation.8 | async-start | bytes 1048576
  237.8 10.2 %slice-start = ((s8[4718592]{0:T(1024)(128)(4,1)}), s8[4194304]{0:T(1024)(128)(4,1)S(1)}, s32[]{:S(2)}) async-start(s8[4718592]{0:T(1024)(128)(4,1)} %bitcast.182), calls=%async_computation.1 | async-start | bytes 8388608
  237.8 10.2 %slice-start.2 = ((s8[4718592]{0:T(1024)(128)(4,1)}), s8[4194304]{0:T(1024)(128)(4,1)S(1)}, s32[]{:S(2)}) async-start(s8[4718592]{0:T(1024)(128)(4,1)} %bitcast.184), calls=%async_computation.3 | async-start | bytes 8388608
  237.8 10.2 %slice-start.1 = ((s8[4718592]{0:T(1024)(128)(4,1)}), s8[524288]{0:T(1024)(128)(4,1)S(1)}, s32[]{:S(2)}) async-start(s8[4718592]{0:T(1024)(128)(4,1)} %bitcast.182), calls=%async_computation.2 | async-start | bytes 1048576
  237.8 10.2 %slice-start.3 = ((s8[4718592]{0:T(1024)(128)(4,1)}), s8[524288]{0:T(1024)(128)(4,1)S(1)}, s32[]{:S(2)}) async-start(s8[4718592]{0:T(1024)(128)(4,1)} %bitcast.184), calls=%async_computation.4 | async-start | bytes 1048576
  237.8 10.2 %copy-start.22 = (f32[2048]{0:T(1024)S(1)}, f32[2048]{0:T(1024)}, u32[]{:S(2)}) copy-start(f32[2048]{0:T(1024)} %param.44) | copy-start | bytes 24580
  237.8 10.2 %copy-start.24 = (f32[2048]{0:T(1024)S(1)}, f32[2048]{0:T(1024)}, u32[]{:S(2)}) copy-start(f32[2048]{0:T(1024)} %param.45) | copy-start | bytes 24580
  293.9 6.1 copy-start.26
  293.9 6.1 copy-start.27
  302.9 45.9 %copy-start.9 = (f32[576,512]{1,0:T(8,128)S(1)}, f32[576,512]{1,0:T(8,128)}, u32[]{:S(2)}) copy-start(f32[576,512]{1,0:T(8,128)} %reshape.546) | copy-start | bytes 3538948
  446.9 44.0 %copy-start.4 = (bf16[2,16,18,512]{3,2,1,0:T(8,128)(2,1)S(1)}, bf16[2,16,18,512]{3,2,1,0:T(8,128)(2,1)}, u32[]{:S(2)}) copy-start(bf16[2,16,18,512]{3,2,1,0:T(8,128)(2,1)} %copy-done.2) | copy-start | bytes 1769476
  490.3 30.8 %copy-start.34 = (f32[512]{0:T(512)}, f32[512]{0:T(512)S(1)}, u32[]{:S(2)}) copy-start(f32[512]{0:T(512)S(1)} %get-tuple-element.211) | copy-start | bytes 6148
  506.2 6.8 copy-start.5
  897.1 15.6 %slice-start.8 = ((s8[6291456]{0:T(1024)(128)(4,1)}), s8[4194304]{0:T(1024)(128)(4,1)S(1)}, s32[]{:S(2)}) async-start(s8[6291456]{0:T(1024)(128)(4,1)} %bitcast.191), calls=%async_computation.9 | async-start | bytes 8388608
  901.9 8.7 copy-start.10
  901.9 10.7 %slice-start.9 = ((s8[6291456]{0:T(1024)(128)(4,1)}), s8[2097152]{0:T(1024)(128)(4,1)S(1)}, s32[]{:S(2)}) async-start(s8[6291456]{0:T(1024)(128)(4,1)} %bitcast.191), calls=%async_computation.10 | async-start | bytes 4194304
  (22 other events, 48.9 us)
Sparse Core Ops, SparseCore 0:
  513.1 383.9 all-reduce.10
where the time goes:
time: 930 us; the launch traced here: 923 us
  waiting for transfers between devices  359 us (39%)
  blocking collectives  244 us (26%)
  local copies, waits for them, and re-layouts  144 us (15%)
  matrix products  122 us (13%)
  other arithmetic  39.1 us (4%)
  between operations  15.2 us (2%)
    psum x1, waiting for transfers between devices, body(): lax.psum((grad_reduce, spatial_flat, grad_expand, head_term), ('task', 'd...  359 us
    psum x3, blocking collectives, norm_forward(): lax.psum((jnp.sum(values * valid, axis=0), jnp.sum(values * values * vali...  123 us
    psum x3, blocking collectives, norm_backward(): lax.psum((jnp.sum(upstream, axis=0), jnp.sum(upstream * normed, axis=0)),...  121 us
    scatter-add x9, local copies, waits for them, and re-layouts, spatial_backward(): grad_pad.at[:, row_tap:row_tap + height, col_tap:col_tap + span]  60.4 us
    unnamed x98, local copies, waits for them, and re-layouts  38 us
    dot_general x9, matrix products, spatial_forward(): jnp.einsum('ihwc,cd->ihwd', window, kernel[row_tap, col_tap], preferred_e...  29.3 us
    dot_general x9, matrix products, spatial_backward(): jnp.einsum('ihwd,cd->ihwc', grad_low, kernel[row_tap, col_tap], preferred...  29.3 us
  transfers between devices with their start and end apart: 1, of which 1 were waited for; matrix products, arithmetic and copies ran while one was open for 3% of the time, Pallas kernels for 0%

commit v1 on v0

v1 whole, which is shorter than its diff:
```python
import functools

import jax
import jax.numpy as jnp
from jax import lax
from jax.experimental import pallas as pl
from jax.experimental.pallas import tpu as pltpu
from jax.sharding import PartitionSpec as P

TASKS = 3
EPS = 1e-05
SOFT = 0.01
MESH = pl.DeviceIdType.MESH
F32 = jnp.float32
LOW = jnp.bfloat16
NT = (((1,), (1,)), ((), ()))
TN = (((0,), (0,)), ((), ()))
SEGMENTS = ("heads", "expand", "spatial", "reduce")


class Plan:
    def __init__(self, mesh, images, w_reduce, w_heads):
        self.tasks = mesh.shape["task"]
        self.dp = mesh.shape["dp"]
        self.line = self.dp // 2
        self.devices = self.tasks * self.dp
        assert self.tasks == 4 and self.dp % 2 == 0
        self.count, self.height, self.span, self.wide = images.shape
        assert self.height & (self.height - 1) == 0 and self.height % 16 == 0
        self.mid = w_reduce.shape[1]
        self.heads = w_heads.shape[1]
        self.image = self.height * self.span
        self.cells = self.count * self.image
        self.step = self.image + self.height
        self.rows = self.count * self.step - self.height
        self.both = 2 * self.count * self.step - self.height
        self.half = self.wide // 2
        unit = self.tasks * self.line * 16
        real = {
            "heads": self.heads // 256 * self.half,
            "expand": self.half // 256 * self.mid,
            "spatial": 9 * self.mid,
            "reduce": self.mid // 256 * self.half,
        }
        self.real = real
        self.size = {k: -(-real[k] // unit) * unit for k in SEGMENTS}
        self.base, at = {}, 0
        for k in SEGMENTS:
            self.base[k] = at
            at += self.size[k]
        self.total = at


def chunk_of(rows):
    for size in (128, 96, 64, 48, 32, 16):
        if rows % size == 0:
            return size
    raise ValueError(rows)


def column_sum(values):
    return jnp.sum(values.reshape(values.shape[0] // 8, 8, values.shape[1]), axis=0)


def fold(part):
    return jnp.sum(part, axis=0, keepdims=True)


def logistic(values):
    return 0.5 + 0.5 * jnp.tanh(0.5 * values)


def lanes(block, width=128):
    return pl.ds(pl.multiple_of(block * width, width), width)


def span16(start, size):
    return pl.ds(pl.multiple_of(start, 16), size)


def repeat(count, body):
    def step(i, carry):
        body(i)
        return carry

    lax.fori_loop(0, count, step, 0)


def block_kernel(
    plan,
    images,
    sizes,
    limits,
    head_grad,
    w_reduce,
    w_spatial,
    w_expand,
    w_heads,
    gain_a,
    shift_a,
    gain_b,
    shift_b,
    gain_c,
    shift_c,
    head_out,
    grad_images,
    gathered,
    gain_a_grad,
    shift_a_grad,
    gain_b_grad,
    shift_b_grad,
    gain_c_grad,
    shift_c_grad,
    *scratch,
):
    (
        img,
        wr,
        ws,
        we,
        wh,
        hg,
        trunk,
        sib_one,
        sib_two,
        img_t,
        merged,
        third,
        first,
        second,
        back,
        hid_a,
        hid_b,
        hid_b_t,
        low_b,
        low_b_all,
        low_a,
        gsc,
        stage,
        mask,
        coef,
        msg,
        slots,
        wide_msg,
        wide_slots,
        total,
        terms,
        recv_one,
        recv_two,
        recv_three,
        load_sem,
        out_sem,
        sum_send,
        sum_recv,
        sib_send,
        sib_recv,
        ring_send,
        ring_recv,
        keep_sem,
    ) = scratch
    p = plan
    n_img, height, image, step = p.count, p.height, p.image, p.step
    cells, rows, mid, wide, half = p.cells, p.rows, p.mid, p.wide, p.half
    mid_blocks, wide_blocks = mid // 128, wide // 128
    task = lax.axis_index("task")
    dp = lax.axis_index("dp")
    core = lax.rem(dp, 2)
    level = dp // 2
    me = task * p.dp + dp
    sibling = {"task": task, "dp": dp + 1 - 2 * core}

    def remote(src, dst, send, recv, device):
        return pltpu.make_async_remote_copy(
            src_ref=src, dst_ref=dst, send_sem=send, recv_sem=recv, device_id=device, device_id_type=MESH
        )

    def take(ref, sem):
        pltpu.make_async_copy(ref, ref, sem).wait()

    barrier = pltpu.get_barrier_semaphore()

    def greet(i):
        other = lax.rem(me + 1 + i, p.devices)
        pl.semaphore_signal(
            barrier,
            inc=1,
            device_id={"task": other // p.dp, "dp": lax.rem(other, p.dp)},
            device_id_type=MESH,
        )

    repeat(p.devices - 1, greet)

    loads = {
        "images": (images, img),
        "reduce": (w_reduce, wr),
        "grad": (head_grad, hg.at[pl.ds(0, cells)]),
        "heads": (w_heads, wh),
        "limits": (limits, trunk),
        "expand": (w_expand, we),
    }
    order = list(loads)
    for i, key in enumerate(order):
        pltpu.make_async_copy(*loads[key], load_sem.at[i]).start()
    for row_tap in range(3):
        for col_tap in range(3):
            pltpu.make_async_copy(
                w_spatial.at[row_tap * 3 + col_tap],
                ws.at[col_tap, pl.ds(row_tap * mid, mid)],
                load_sem.at[len(order)],
            ).start()

    def loaded(key):
        pltpu.make_async_copy(*loads[key], load_sem.at[order.index(key)]).wait()

    mask[...] = jnp.zeros_like(mask)
    for k in range(n_img):
        at = lax.broadcasted_iota(jnp.int32, (image, 128), 0)
        inside = ((at & (height - 1)) < sizes[k, 0]) & ((at // height) < sizes[k, 1])
        mask[pl.ds(k * step, image)] = jnp.where(inside, 1.0, 0.0)
    zero_rows = jnp.zeros((height, 3 * mid), LOW)
    for k in range(2 * n_img + 1):
        hid_a[pl.ds(k * step, height)] = zero_rows
    for k in range(n_img + 1):
        low_b[pl.ds(k * step, height)] = zero_rows
    low_b_all[pl.ds(rows, height)] = jnp.zeros((height, mid // 2), LOW)

    def sum_start(k, slot):
        slots[slot, me] = msg[k]

        def send(i):
            other = lax.rem(me + 1 + i, p.devices)
            remote(
                msg.at[k],
                slots.at[slot, me],
                sum_send.at[k],
                sum_recv.at[k],
                {"task": other // p.dp, "dp": lax.rem(other, p.dp)},
            ).start()

        repeat(p.devices - 1, send)

    def sum_finish(k, slot):
        some = slots.at[slot, pl.ds(0, p.devices - 1)]
        take(some, sum_recv.at[k])
        take(some, sum_send.at[k])
        total[pl.ds(0, 2 * mid_blocks)] = jnp.sum(slots[slot], axis=0)

    plane = 2 * p.tasks
    spot = task * 2 + core

    def wide_start(k):
        wide_slots[k, spot] = wide_msg[k, 0]
        for i in range(1, plane):
            other = lax.rem(spot + i, plane)
            remote(
                wide_msg.at[k, 0],
                wide_slots.at[k, spot],
                sum_send.at[5 + 2 * k],
                sum_recv.at[5 + 2 * k],
                {"task": other // 2, "dp": level * 2 + lax.rem(other, 2)},
            ).start()

    def wide_turn(k):
        some = wide_slots.at[k, pl.ds(0, plane - 1)]
        take(some, sum_recv.at[5 + 2 * k])
        take(some, sum_send.at[5 + 2 * k])
        partial = jnp.sum(wide_slots[k, pl.ds(0, plane)], axis=0)
        wide_msg[k, 1] = partial
        wide_slots[k, plane + level] = partial
        for i in range(1, p.line):
            other = lax.rem(level + i, p.line)
            remote(
                wide_msg.at[k, 1],
                wide_slots.at[k, plane + level],
                sum_send.at[6 + 2 * k],
                sum_recv.at[6 + 2 * k],
                {"task": task, "dp": other * 2 + core},
            ).start()

    def wide_finish(k):
        some = wide_slots.at[k, pl.ds(plane, p.line - 1)]
        take(some, sum_recv.at[6 + 2 * k])
        take(some, sum_send.at[6 + 2 * k])
        total[...] = jnp.sum(wide_slots[k, pl.ds(plane, p.line)], axis=0)

    low_bit, high_bit = lax.rem(task, 2), task // 2
    near = {"task": task + 1 - 2 * low_bit, "dp": dp}
    far = {"task": task + 2 - 4 * high_bit, "dp": dp}
    routes = ((low_bit, high_bit, near, far), (high_bit, low_bit, far, near))

    def ring(name, stage_at, part):
        s = SEGMENTS.index(name)
        return ring_send.at[s, stage_at, part], ring_recv.at[s, stage_at, part]

    def put(name, row, values):
        low = values.astype(LOW)
        at = span16(p.base[name] + row, low.shape[0])
        terms[0, at, :] = low[:, :128]
        terms[1, at, :] = low[:, 128:]

    def add(part, to, others, count):
        size = chunk_of(count)

        def one(i):
            at = span16(to + i * size, size)
            acc = terms[part, at, :].astype(F32)
            for read in others:
                acc = acc + read(i * size, size)
            terms[part, at, :] = acc.astype(LOW)

        repeat(count // size, one)

    def from_one(name, part, start):
        return lambda i, size: recv_one[part, span16(p.base[name] // 2 + start + i, size), :].astype(F32)

    def from_two(name, part):
        return lambda i, size: recv_two[part, span16(p.base[name] // 4 + i, size), :].astype(F32)

    def from_three(name, part, k):
        return lambda i, size: recv_three[
            part, k, span16(p.base[name] // (4 * p.line) + i, size), :
        ].astype(F32)

    def send_one(name):
        size = p.size[name] // 2
        for part, (mine, _, partner, _) in enumerate(routes):
            send, recv = ring(name, 0, part)
            remote(
                terms.at[part, span16(p.base[name] + (1 - mine) * size, size)],
                recv_one.at[part, pl.ds(p.base[name] // 2, size)],
                send,
                recv,
                partner,
            ).start()

    def send_two(name):
        size = p.size[name] // 4
        for part, (mine, then, _, partner) in enumerate(routes):
            send, recv = ring(name, 0, part)
            some = recv_one.at[part, pl.ds(p.base[name] // 2, 2 * size)]
            take(some, recv)
            take(some, send)
            at = p.base[name] + mine * 2 * size + (1 - then) * size
            add(part, at, [from_one(name, part, (1 - then) * size)], size)
            send, recv = ring(name, 1, part)
            remote(
                terms.at[part, span16(at, size)],
                recv_two.at[part, pl.ds(p.base[name] // 4, size)],
                send,
                recv,
                partner,
            ).start()

    def quarter(name, part):
        mine, then, _, _ = routes[part]
        return p.base[name] + (mine * 2 + then) * (p.size[name] // 4)

    def send_three(name):
        size = p.size[name] // 4
        piece = size // p.line
        for part, (mine, then, _, _) in enumerate(routes):
            send, recv = ring(name, 1, part)
            some = recv_two.at[part, pl.ds(p.base[name] // 4, size)]
            take(some, recv)
            take(some, send)
            at = quarter(name, part)
            add(part, at, [from_one(name, part, then * size), from_two(name, part)], size)
            send, recv = ring(name, 2, part)
            for i in range(1, p.line):
                other = lax.rem(level + i, p.line)
                remote(
                    terms.at[part, span16(at + other * piece, piece)],
                    recv_three.at[part, i - 1, pl.ds(p.base[name] // (4 * p.line), piece)],
                    send,
                    recv,
                    {"task": task, "dp": other * 2 + core},
                ).start()

    def home(name, part, start, size):
        return gathered.at[core, part, span16(start, size)]

    def gather_one(name):
        s = SEGMENTS.index(name)
        piece = p.size[name] // 4 // p.line
        for part in range(2):
            send, recv = ring(name, 2, part)
            some = recv_three.at[part, pl.ds(0, p.line - 1), pl.ds(p.base[name] // (4 * p.line), piece)]
            take(some, recv)
            take(some, send)
            at = quarter(name, part) + level * piece
            add(part, at, [from_three(name, part, k) for k in range(p.line - 1)], piece)
            send, recv = ring(name, 3, part)
            mine = terms.at[part, span16(at, piece)]
            for i in range(1, p.line):
                other = lax.rem(level + i, p.line)
                target = {"task": task, "dp": other * 2 + core}
                remote(mine, home(name, part, at, piece), send, recv, target).start()
            pltpu.make_async_copy(mine, home(name, part, at, piece), keep_sem.at[s, part]).start()

    def gather_two(name):
        s = SEGMENTS.index(name)
        size = p.size[name] // 4
        piece = size // p.line
        for part, (_, _, _, partner) in enumerate(routes):
            send, recv = ring(name, 3, part)
            some = recv_three.at[part, pl.ds(0, p.line - 1), pl.ds(p.base[name] // (4 * p.line), piece)]
            take(some, recv)
            take(some, send)
            at = quarter(name, part)
            take(terms.at[part, span16(at, piece)], keep_sem.at[s, part])
            mine = home(name, part, at, size)
            send, recv = ring(name, 4, part)
            remote(mine, mine, send, recv, partner).start()

    def gather_three(name):
        size = p.size[name] // 2
        for part, (mine, _, partner, _) in enumerate(routes):
            send, recv = ring(name, 4, part)
            some = recv_two.at[part, pl.ds(p.base[name] // 4, size // 2)]
            take(some, recv)
            take(some, send)
            ours = home(name, part, p.base[name] + mine * size, size)
            send, recv = ring(name, 5, part)
            remote(ours, ours, send, recv, partner).start()

    def gather_four(name):
        for part in range(2):
            send, recv = ring(name, 5, part)
            some = recv_one.at[part, pl.ds(p.base[name] // 2, p.size[name] // 2)]
            take(some, recv)
            take(some, send)
            send, recv = ring(name, 6, part)
            ours = home(name, part, p.base[name], p.size[name])
            remote(ours, ours, send, recv, sibling).start()

    def gather_end(name):
        for part in range(2):
            send, recv = ring(name, 6, part)
            some = terms.at[part, pl.ds(p.base[name], p.size[name])]
            take(some, send)
            take(some, recv)

    other_half = pl.ds(pl.multiple_of((1 - core) * half, 128), half)
    other_quarter = pl.ds(pl.multiple_of(mid + (1 - core) * (mid // 2), 128), mid // 2)
    swaps = (
        (images.at[:, other_half], sib_one),
        (head_grad, hg.at[pl.ds(cells, cells)]),
        (hid_a.at[pl.ds(height, rows)], hid_a.at[pl.ds(n_img * step + height, rows)]),
        (hid_b.at[pl.ds(0, cells)], hid_b.at[pl.ds(cells, cells)]),
        (trunk.at[:, other_half], sib_two),
        (trunk.at[:, other_half], sib_one),
        (low_b.at[pl.ds(height, rows), other_quarter], low_b_all.at[pl.ds(rows + height, rows)]),
        (low_a.at[pl.ds(0, cells)], low_a.at[pl.ds(cells, cells)]),
    )

    def swap(k):
        src, dst = swaps[k]
        return remote(src, dst, sib_send.at[k], sib_recv.at[k], sibling)

    msg[0] = jnp.broadcast_to(fold(column_sum(mask[...])), (2 * mid_blocks, 128))
    pl.semaphore_wait(barrier, p.devices - 1)
    sum_start(0, 0)
    swap(0).start()
    swap(1).start()

    def put_stats(ref, at, blocks, block, one, two):
        ref[(*at, pl.ds(block, 1))] = fold(one)
        ref[(*at, pl.ds(blocks + block, 1))] = fold(two)

    loaded("images")
    loaded("reduce")

    def first_layer(nb):
        values = jnp.dot(img[...], wr[:, lanes(nb, 256)], preferred_element_type=F32)
        for h in range(2):
            one = two = jnp.zeros((8, 128), F32)
            for k in range(n_img):
                at = pl.ds(k * image, image)
                part = values[k * image : (k + 1) * image, h * 128 : h * 128 + 128]
                part = part * mask[pl.ds(k * step, image)]
                first[at, lanes(2 * nb + h)] = part
                one = one + column_sum(part)
                two = two + column_sum(part * part)
            put_stats(msg, (1,), mid_blocks, 2 * nb + h, one, two)

    repeat(mid // 256, first_layer)
    sum_finish(0, 0)
    count = total[pl.ds(0, 1)]
    sum_start(1, 1)

    loaded("grad")
    loaded("heads")
    loaded("limits")
    head = p.heads // TASKS

    def merge(nb):
        at_wide = pl.ds(pl.multiple_of(nb * 256, 256), 256)
        for t in range(TASKS):
            at_head = pl.ds(t * head, head)
            values = lax.dot_general(
                hg[pl.ds(0, cells), at_head], wh[at_wide, at_head], NT, preferred_element_type=F32
            )
            gsc[t] = values.astype(LOW)

        def drop(i):
            at = span16(i * 64, 64)
            for h in range(2):
                grads = [gsc[t, at, pl.ds(h * 128, 128)].astype(F32) for t in range(TASKS)]
                signed, size, kept = 0.0, 0.0, 0.0
                for g in grads:
                    square = g * g + SOFT
                    signed = signed + g
                    size = size + square * lax.rsqrt(square)
                    kept = kept + jnp.tanh(g * 5.0) * g
                limit = trunk[at, lanes(2 * nb + h)].astype(F32)
                lean = jnp.tanh(2.5 + 2.5 * (signed / size) - 5.0 * limit)
                merged[at, lanes(2 * nb + h)] = 0.5 * (signed + lean * kept)

        repeat(cells // 64, drop)

    repeat(wide // 256, merge)
    swap(0).wait_recv()

    def turn_images(j):
        own = img[:, pl.ds(pl.multiple_of(core * half + j * 128, 128), 128)]
        both = jnp.concatenate([own, sib_one[:, lanes(j)]], axis=0)
        img_t[lanes(j), :] = both.T

    def center(blocks):
        mean = total[pl.ds(0, blocks)] / count
        spread = total[pl.ds(blocks, blocks)] / count - mean * mean + EPS
        coef[0, pl.ds(0, blocks)] = mean
        coef[1, pl.ds(0, blocks)] = lax.rsqrt(spread)

    def row(k, block):
        return coef[k, pl.ds(block, 1)]

    def edges():
        at = lax.broadcasted_iota(jnp.int32, (image, 128), 0) & (height - 1)
        return at != 0, at != height - 1

    def put_shifted(ref, start, block, values, above, below):
        at = pl.ds(start, image)
        up = jnp.where(above, pltpu.roll(values, 1, 0), 0.0)
        down = jnp.where(below, pltpu.roll(values, image - 1, 0), 0.0)
        for h, part in enumerate((up, values, down)):
            ref[at, pl.ds(pl.multiple_of(h * mid + block * 128, 128), 128)] = part.astype(LOW)

    sum_finish(1, 1)
    center(mid_blocks)
    coef[2, pl.ds(0, mid_blocks)] = coef[1, pl.ds(0, mid_blocks)]

    def normalize_a(cb):
        above, below = edges()
        gain, shift = gain_a[pl.ds(cb, 1)], shift_a[pl.ds(cb, 1)]
        for k in range(n_img):
            at = pl.ds(k * image, image)
            hat = (first[at, lanes(cb)] - row(0, cb)) * row(1, cb)
            first[at, lanes(cb)] = hat
            pre = hat * gain + shift
            hidden = pre * logistic(pre) * mask[pl.ds(k * step, image)]
            put_shifted(hid_a, height + k * step, cb, hidden, above, below)

    repeat(mid_blocks, normalize_a)
    swap(2).start()

    take(ws, load_sem.at[len(order)])

    def second_layer(nb):
        values = None
        for j in range(3):
            term = jnp.dot(
                hid_a[pl.ds(j * height, rows)], ws[j, :, lanes(nb, 256)], preferred_element_type=F32
            )
            values = term if values is None else values + term
        for h in range(2):
            part = values[:, h * 128 : h * 128 + 128] * mask[...]
            second[:, lanes(2 * nb + h)] = part
            put_stats(msg, (2,), mid_blocks, 2 * nb + h, column_sum(part), column_sum(part * part))

    repeat(mid // 256, second_layer)
    sum_start(2, 0)
    repeat(half // 128, turn_images)
    sum_finish(2, 0)
    center(mid_blocks)
    coef[3, pl.ds(0, mid_blocks)] = coef[1, pl.ds(0, mid_blocks)]

    def normalize_b(cb):
        gain, shift = gain_b[pl.ds(cb, 1)], shift_b[pl.ds(cb, 1)]
        for k in range(n_img):
            at = pl.ds(k * step, image)
            hat = (second[at, lanes(cb)] - row(0, cb)) * row(1, cb)
            second[at, lanes(cb)] = hat
            pre = hat * gain + shift
            hidden = pre * logistic(pre) * mask[at]
            hid_b[pl.ds(k * image, image), lanes(cb)] = hidden.astype(LOW)

    repeat(mid_blocks, normalize_b)
    swap(3).start()

    loaded("expand")

    def third_layer(nb):
        values = jnp.dot(hid_b[pl.ds(0, cells)], we[:, lanes(nb, 256)], preferred_element_type=F32)
        third[:, lanes(nb, 256)] = values
        for h in range(2):
            part = values[:, h * 128 : h * 128 + 128]
            put_stats(
                wide_msg, (0, 0), wide_blocks, 2 * nb + h, column_sum(part), column_sum(part * part)
            )

    repeat(wide // 256, third_layer)
    wide_start(0)
    swap(3).wait_recv()
    wide_turn(0)

    def turn_hidden(j):
        hid_b_t[lanes(j), :] = hid_b[:, lanes(j)].T

    repeat(mid_blocks, turn_hidden)
    wide_finish(0)
    center(wide_blocks)

    chunk = chunk_of(image)

    def normalize_c(cb):
        gain, shift = gain_c[pl.ds(cb, 1)], shift_c[pl.ds(cb, 1)]
        one = two = jnp.zeros((8, 128), F32)
        for k in range(n_img):
            for r in range(image // chunk):
                at = pl.ds(k * image + r * chunk, chunk)
                valid = mask[pl.ds(k * step + r * chunk, chunk)]
                hat = (third[at, lanes(cb)] - row(0, cb)) * row(1, cb)
                third[at, lanes(cb)] = hat
                pre = hat * gain + shift + img[at, lanes(cb)].astype(F32)
                gate = logistic(pre)
                trunk[at, lanes(cb)] = (pre * gate * valid).astype(LOW)
                up = merged[at, lanes(cb)] * (gate * (1.0 + pre * (1.0 - gate))) * valid
                merged[at, lanes(cb)] = up
                one = one + column_sum(up)
                two = two + column_sum(up * hat)
        put_stats(wide_msg, (1, 0), wide_blocks, cb, one, two)

    repeat(wide_blocks, normalize_c)
    wide_start(1)
    swap(4).start()

    def head_layer(nb):
        values = jnp.dot(trunk[...], wh[:, lanes(nb, 256)], preferred_element_type=F32)
        stage[:, lanes(nb, 256)] = values.astype(LOW)

    repeat(p.heads // 256, head_layer)
    pltpu.make_async_copy(stage, head_out, out_sem.at[0]).start()
    wide_turn(1)
    swap(1).wait_recv()
    swap(4).wait_recv()

    def heads_gradient(j):
        own = trunk[:, pl.ds(pl.multiple_of(core * half + j * 256, 128), 256)]
        both = jnp.concatenate([own, sib_two[:, lanes(j, 256)]], axis=0)
        values = lax.dot_general(both, hg[...], TN, preferred_element_type=F32)
        for b in range(p.heads // 256):
            put("heads", b * half + j * 256, values[:, b * 256 : b * 256 + 256])

    repeat(half // 256, heads_gradient)
    send_one("heads")
    swap(4).wait_send()
    wide_finish(1)

    def backward(blocks, gain, inverse):
        scale = gain * inverse
        coef[4, pl.ds(0, blocks)] = scale
        coef[5, pl.ds(0, blocks)] = -scale * total[pl.ds(0, blocks)] / count
        coef[6, pl.ds(0, blocks)] = -scale * total[pl.ds(blocks, blocks)] / count

    shift_c_grad[...] = total[pl.ds(0, wide_blocks)]
    gain_c_grad[...] = total[pl.ds(wide_blocks, wide_blocks)]
    backward(wide_blocks, gain_c[...], coef[1])

    def third_gradient(cb):
        for k in range(n_img):
            for r in range(image // chunk):
                at = pl.ds(k * image + r * chunk, chunk)
                valid = mask[pl.ds(k * step + r * chunk, chunk)]
                down = merged[at, lanes(cb)] * row(4, cb) + row(5, cb) + third[at, lanes(cb)] * row(6, cb)
                trunk[at, lanes(cb)] = (down * valid).astype(LOW)

    repeat(wide_blocks, third_gradient)
    swap(5).start()

    def slope_of(pre):
        gate = logistic(pre)
        return gate * (1.0 + pre * (1.0 - gate))

    def third_back(nb):
        values = lax.dot_general(trunk[...], we[lanes(nb, 256), :], NT, preferred_element_type=F32)
        for h in range(2):
            cb = 2 * nb + h
            one = two = jnp.zeros((8, 128), F32)
            for k in range(n_img):
                at = pl.ds(k * image, image)
                hat = second[pl.ds(k * step, image), lanes(cb)]
                pre = hat * gain_b[pl.ds(cb, 1)] + shift_b[pl.ds(cb, 1)]
                up = values[k * image : (k + 1) * image, h * 128 : h * 128 + 128]
                up = up * slope_of(pre) * mask[pl.ds(k * step, image)]
                back[at, lanes(cb)] = up
                one = one + column_sum(up)
                two = two + column_sum(up * hat)
            put_stats(msg, (3,), mid_blocks, cb, one, two)

    repeat(mid // 256, third_back)
    sum_start(3, 1)
    send_two("heads")
    swap(5).wait_recv()

    def expand_gradient(j):
        own = trunk[:, pl.ds(pl.multiple_of(core * half + j * 256, 128), 256)]
        both = jnp.concatenate([own, sib_one[:, lanes(j, 256)]], axis=0)
        put("expand", j * mid, jnp.dot(hid_b_t[...], both, preferred_element_type=F32))

    repeat(half // 256, expand_gradient)
    send_one("expand")
    sum_finish(3, 1)
    shift_b_grad[...] = total[pl.ds(0, mid_blocks)]
    gain_b_grad[...] = total[pl.ds(mid_blocks, mid_blocks)]
    backward(mid_blocks, gain_b[...], coef[3, pl.ds(0, mid_blocks)])

    def second_gradient(cb):
        above, below = edges()
        for k in range(n_img):
            at = pl.ds(k * step, image)
            down = back[pl.ds(k * image, image), lanes(cb)] * row(4, cb) + row(5, cb)
            down = (down + second[at, lanes(cb)] * row(6, cb)) * mask[at]
            put_shifted(low_b, height + k * step, cb, down, above, below)

    repeat(mid_blocks, second_gradient)
    swap(6).start()
    own_quarter = pl.ds(pl.multiple_of(mid + core * (mid // 2), 128), mid // 2)
    low_b_all[pl.ds(0, rows)] = low_b[pl.ds(height, rows), own_quarter]

    def second_back(nb):
        values = None
        for i in range(3):
            for j in range(3):
                term = lax.dot_general(
                    low_b[pl.ds((2 - j) * height, rows), pl.ds((2 - i) * mid, mid)],
                    ws[j, pl.ds(pl.multiple_of(i * mid + nb * 256, 256), 256), :],
                    NT,
                    preferred_element_type=F32,
                )
                values = term if values is None else values + term
        for h in range(2):
            cb = 2 * nb + h
            one = two = jnp.zeros((8, 128), F32)
            for k in range(n_img):
                at = pl.ds(k * image, image)
                hat = first[at, lanes(cb)]
                pre = hat * gain_a[pl.ds(cb, 1)] + shift_a[pl.ds(cb, 1)]
                up = values[k * step : k * step + image, h * 128 : h * 128 + 128]
                up = up * slope_of(pre) * mask[pl.ds(k * step, image)]
                back[at, lanes(cb)] = up
                one = one + column_sum(up)
                two = two + column_sum(up * hat)
            put_stats(msg, (4,), mid_blocks, cb, one, two)

    repeat(mid // 256, second_back)
    sum_start(4, 0)
    send_three("heads")
    send_two("expand")
    swap(2).wait_recv()
    swap(6).wait_recv()

    def spatial_gradient(i):
        per = 3 * mid // 256
        j, k = i // per, lax.rem(i, per)
        row_tap, sub = k // (mid // 256), lax.rem(k, mid // 256)
        values = lax.dot_general(
            hid_a[span16(j * height, p.both), lanes(k, 256)],
            low_b_all[...],
            TN,
            preferred_element_type=F32,
        )
        put("spatial", (row_tap * 3 + j) * mid + sub * 256, values)

    repeat(9 * mid // 256, spatial_gradient)
    send_one("spatial")
    sum_finish(4, 0)
    shift_a_grad[...] = total[pl.ds(0, mid_blocks)]
    gain_a_grad[...] = total[pl.ds(mid_blocks, mid_blocks)]
    backward(mid_blocks, gain_a[...], coef[2, pl.ds(0, mid_blocks)])

    def first_gradient(cb):
        for k in range(n_img):
            at = pl.ds(k * image, image)
            down = back[at, lanes(cb)] * row(4, cb) + row(5, cb) + first[at, lanes(cb)] * row(6, cb)
            low_a[at, lanes(cb)] = (down * mask[pl.ds(k * step, image)]).astype(LOW)

    repeat(mid_blocks, first_gradient)
    swap(7).start()
    gather_one("heads")
    send_three("expand")
    swap(7).wait_recv()

    def reduce_gradient(i):
        j, b = i // (mid // 256), lax.rem(i, mid // 256)
        values = jnp.dot(img_t[lanes(j, 256), :], low_a[:, lanes(b, 256)], preferred_element_type=F32)
        put("reduce", b * half + j * 256, values)

    repeat(half // 256 * (mid // 256), reduce_gradient)
    send_one("reduce")
    send_two("spatial")

    def first_back(nb):
        values = lax.dot_general(low_a[pl.ds(0, cells)], wr[lanes(nb, 256), :], NT, preferred_element_type=F32)
        for h in range(2):
            for k in range(n_img):
                at = pl.ds(k * image, image)
                part = values[k * image : (k + 1) * image, h * 128 : h * 128 + 128]
                part = (part + merged[at, lanes(2 * nb + h)]) * mask[pl.ds(k * step, image)]
                img[at, lanes(2 * nb + h)] = part.astype(LOW)

    repeat(wide // 256, first_back)
    pltpu.make_async_copy(img, grad_images, out_sem.at[1]).start()

    gather_two("heads")
    gather_one("expand")
    send_two("reduce")
    gather_three("heads")
    gather_two("expand")
    send_three("spatial")
    gather_four("heads")
    send_three("reduce")
    gather_three("expand")
    gather_one("spatial")
    gather_four("expand")
    gather_one("reduce")
    gather_two("spatial")
    gather_two("reduce")
    gather_three("spatial")
    gather_three("reduce")
    gather_four("spatial")
    gather_four("reduce")
    for name in SEGMENTS:
        gather_end(name)
    pltpu.make_async_copy(stage, head_out, out_sem.at[0]).wait()
    pltpu.make_async_copy(img, grad_images, out_sem.at[1]).wait()
    for k in (0, 1, 2, 3, 5, 6, 7):
        swap(k).wait_send()


def run_block(plan, *arrays):
    p = plan
    cells, rows, mid, wide, half = p.cells, p.rows, p.mid, p.wide, p.half
    mid_blocks, wide_blocks = mid // 128, wide // 128
    anywhere = pl.BlockSpec(memory_space=pl.ANY)
    vmem = pl.BlockSpec(memory_space=pltpu.VMEM)
    smem = pl.BlockSpec(memory_space=pltpu.SMEM)
    shape = jax.ShapeDtypeStruct
    scratch = [
        pltpu.VMEM((cells, wide), LOW),
        pltpu.VMEM((wide, mid), LOW),
        pltpu.VMEM((3, 3 * mid, mid), LOW),
        pltpu.VMEM((mid, wide), LOW),
        pltpu.VMEM((wide, p.heads), LOW),
        pltpu.VMEM((2 * cells, p.heads), LOW),
        pltpu.VMEM((cells, wide), LOW),
        pltpu.VMEM((cells, half), LOW),
        pltpu.VMEM((cells, half), LOW),
        pltpu.VMEM((half, 2 * cells), LOW),
        pltpu.VMEM((cells, wide), F32),
        pltpu.VMEM((cells, wide), F32),
        pltpu.VMEM((cells, mid), F32),
        pltpu.VMEM((rows, mid), F32),
        pltpu.VMEM((cells, mid), F32),
        pltpu.VMEM((p.both + 2 * p.height, 3 * mid), LOW),
        pltpu.VMEM((2 * cells, mid), LOW),
        pltpu.VMEM((mid, 2 * cells), LOW),
        pltpu.VMEM((rows + 2 * p.height, 3 * mid), LOW),
        pltpu.VMEM((p.both, mid // 2), LOW),
        pltpu.VMEM((2 * cells, mid), LOW),
        pltpu.VMEM((TASKS, cells, 256), LOW),
        pltpu.VMEM((cells, p.heads), LOW),
        pltpu.VMEM((rows, 128), F32),
        pltpu.VMEM((7, wide_blocks, 128), F32),
        pltpu.VMEM((5, 2 * mid_blocks, 128), F32),
        pltpu.VMEM((2, p.devices, 2 * mid_blocks, 128), F32),
        pltpu.VMEM((2, 2, 2 * wide_blocks, 128), F32),
        pltpu.VMEM((2, 2 * p.tasks + p.line, 2 * wide_blocks, 128), F32),
        pltpu.VMEM((2 * wide_blocks, 128), F32),
        pltpu.VMEM((2, p.total, 128), LOW),
        pltpu.VMEM((2, p.total // 2, 128), LOW),
        pltpu.VMEM((2, p.total // 4, 128), LOW),
        pltpu.VMEM((2, p.line - 1, p.total // (4 * p.line), 128), LOW),
        pltpu.SemaphoreType.DMA((7,)),
        pltpu.SemaphoreType.DMA((2,)),
        pltpu.SemaphoreType.DMA((9,)),
        pltpu.SemaphoreType.DMA((9,)),
        pltpu.SemaphoreType.DMA((8,)),
        pltpu.SemaphoreType.DMA((8,)),
        pltpu.SemaphoreType.DMA((4, 7, 2)),
        pltpu.SemaphoreType.DMA((4, 7, 2)),
        pltpu.SemaphoreType.DMA((4, 2)),
    ]
    return pl.pallas_call(
        functools.partial(block_kernel, plan),
        out_shape=(
            shape((cells, p.heads), LOW),
            shape((cells, wide), LOW),
            shape((2, 2, p.total, 128), LOW),
            shape((mid_blocks, 128), F32),
            shape((mid_blocks, 128), F32),
            shape((mid_blocks, 128), F32),
            shape((mid_blocks, 128), F32),
            shape((wide_blocks, 128), F32),
            shape((wide_blocks, 128), F32),
        ),
        in_specs=[anywhere, smem] + [anywhere] * 6 + [vmem] * 6,
        out_specs=[anywhere] * 3 + [vmem] * 6,
        scratch_shapes=scratch,
        compiler_params=pltpu.CompilerParams(
            collective_id=0, has_side_effects=True, vmem_limit_bytes=63 * 2**20
        ),
        name="block",
    )(*arrays)


def widen_kernel(plan, *refs):
    p = plan
    gathered, heads_in, images_in = refs[:3]
    small_in = refs[3:9]
    heads_out, images_out, out_reduce, out_spatial, out_expand, out_heads = refs[9:15]
    small_out = refs[15:21]
    low, reduce, spatial, expand, heads, heads_low, images_low, load_sem, out_sem, pass_sem = refs[21:]
    fetches = (
        pltpu.make_async_copy(heads_in, heads_low, pass_sem.at[0, 0]),
        pltpu.make_async_copy(images_in, images_low, pass_sem.at[1, 0]),
    )
    passes = (
        pltpu.make_async_copy(heads_low, heads_out, pass_sem.at[0, 1]),
        pltpu.make_async_copy(images_low, images_out, pass_sem.at[1, 1]),
    )
    for one in fetches:
        one.start()
    loads = []
    for s, name in enumerate(SEGMENTS):
        for core in range(2):
            at = (core, slice(None), pl.ds(p.base[name], p.real[name]))
            load = pltpu.make_async_copy(gathered.at[at], low.at[at], load_sem.at[s, core])
            load.start()
            loads.append(load)
    for fetch, one in zip(fetches, passes):
        fetch.wait()
        one.start()
    for src, dst in zip(small_in, small_out):
        dst[...] = src[...]
    where = {
        "heads": (heads, out_heads, p.half, p.heads, True),
        "expand": (expand, out_expand, p.mid, p.half, False),
        "spatial": (spatial, out_spatial, 9 * p.mid, p.mid // 2, False),
        "reduce": (reduce, out_reduce, p.half, p.mid, True),
    }
    copies = []
    for s, name in enumerate(SEGMENTS):
        wide, out, height, width, by_rows = where[name]
        for core in range(2):
            loads[2 * s + core].wait()
            size = 256
            row_at = core * height if by_rows else 0
            col_at = 0 if by_rows else core * width

            def one(i, name=name, wide=wide, out=out, row_at=row_at, col_at=col_at, s=s, core=core):
                rows = pl.ds(pl.multiple_of(row_at + i * size, size), size)
                for b in range(width // 256):
                    src = pl.ds(pl.multiple_of(p.base[name] + b * height + i * size, size), size)
                    for part in range(2):
                        cols = pl.ds(col_at + b * 256 + part * 128, 128)
                        wide[rows, cols] = low[core, part, src, :].astype(F32)
                at = (rows, pl.ds(col_at, width))
                pltpu.make_async_copy(wide.at[at], out.at[at], out_sem.at[s, core]).start()

            repeat(height // size, one)
            at = (pl.ds(row_at, height), pl.ds(col_at, width))
            copies.append(pltpu.make_async_copy(wide.at[at], out.at[at], out_sem.at[s, core]))
    for one in copies + list(passes):
        one.wait()


def widen(plan, head_out, grad_images, gathered, *small):
    p = plan
    anywhere = pl.BlockSpec(memory_space=pl.ANY)
    vmem = pl.BlockSpec(memory_space=pltpu.VMEM)
    shape = jax.ShapeDtypeStruct
    full = ((p.wide, p.mid), (9 * p.mid, p.mid), (p.mid, p.wide), (p.wide, p.heads))
    return pl.pallas_call(
        functools.partial(widen_kernel, plan),
        out_shape=(
            shape(head_out.shape, LOW),
            shape(grad_images.shape, LOW),
            *(shape(one, F32) for one in full),
            *(shape(one.shape, F32) for one in small),
        ),
        in_specs=[anywhere] * 3 + [vmem] * 6,
        out_specs=[anywhere] * 6 + [vmem] * 6,
        scratch_shapes=[
            pltpu.VMEM(gathered.shape, LOW),
            *(pltpu.VMEM(one, F32) for one in full),
            pltpu.VMEM(head_out.shape, LOW),
            pltpu.VMEM(grad_images.shape, LOW),
            pltpu.SemaphoreType.DMA((4, 2)),
            pltpu.SemaphoreType.DMA((4, 2)),
            pltpu.SemaphoreType.DMA((2, 2)),
        ],
        compiler_params=pltpu.CompilerParams(vmem_limit_bytes=56 * 2**20),
        name="widen",
    )(gathered, head_out, grad_images, *small)


def solution(mesh):
    cells_spec = P(("task", "dp"), None, None, None)

    def body(
        images,
        sizes,
        limits,
        head_grad,
        w_reduce,
        w_spatial,
        w_expand,
        w_heads,
        gain_a,
        shift_a,
        gain_b,
        shift_b,
        gain_c,
        shift_c,
    ):
        plan = Plan(mesh, images, w_reduce, w_heads)

        def flat(array):
            return array.transpose(0, 2, 1, 3).reshape(plan.cells, array.shape[3])

        def unflat(array):
            full = (plan.count, plan.span, plan.height, array.shape[1])
            return array.reshape(full).transpose(0, 2, 1, 3)

        outs = run_block(
            plan,
            flat(images),
            sizes,
            flat(limits),
            flat(head_grad),
            w_reduce,
            w_spatial.reshape(9, plan.mid, plan.mid),
            w_expand,
            w_heads,
            *(v.reshape(-1, 128) for v in (gain_a, shift_a, gain_b, shift_b, gain_c, shift_c)),
        )
        outs = widen(plan, *outs)
        return (
            unflat(outs[0]),
            unflat(outs[1]),
            outs[2],
            outs[3].reshape(w_spatial.shape),
            outs[4],
            outs[5],
            *(v.reshape(-1) for v in outs[6:]),
        )

    return jax.shard_map(
        body,
        mesh=mesh,
        in_specs=(cells_spec, P(("task", "dp"), None), cells_spec, cells_spec) + (P(),) * 10,
        out_specs=(cells_spec, cells_spec) + (P(),) * 10,
        check_vma=False,
    )
```

time: 930 us -> 198 us (0.21)
  waiting for transfers between devices: 359 us -> 0 us
  blocking collectives: 244 us -> 0 us
  Pallas kernels: 0 us -> 197 us
  local copies, waits for them, and re-layouts: 144 us -> 0 us
  matrix products: 122 us -> 0 us
  other arithmetic: 39.1 us -> 0 us
  between operations: 15.2 us -> 0.66 us
    psum x1 -> x0, waiting for transfers between devices: 359 us -> none  [body(): lax.psum((grad_reduce, spatial_flat, grad_expand, head_term), ('task', 'd...]
    psum x6 -> x0, blocking collectives: 244 us -> none  [the longest x3 123 us: norm_forward(): lax.psum((jnp.sum(values * valid, axis=0), jnp.sum(values * values * vali...]
    pallas_call x0 -> x2, Pallas kernels: none -> 197 us  [the longest x1 181 us: run_block(): pl.pallas_call(functools.partial(block_kernel, plan), out_shape=(shape((c...]
    dot_general x36 -> x0, matrix products: 122 us -> none  [the longest x9 29.3 us: spatial_forward(): jnp.einsum('ihwc,cd->ihwd', window, kernel[row_tap, col_tap], preferred_e...]
    scatter-add x9 -> x0, local copies, waits for them, and re-layouts: 60.4 us -> none  [spatial_backward(): grad_pad.at[:, row_tap:row_tap + height, col_tap:col_tap + span]]
    unnamed x98 -> x0, local copies, waits for them, and re-layouts: 38 us -> none
    convert_element_type x5 -> x0, local copies, waits for them, and re-layouts: 23 us -> none  [the longest x2 11.5 us: body(): limits = thresholds.reshape(pixels, wide).astype(jnp.float32)]
    reduce_sum x4 -> x0, other arithmetic: 19.4 us -> none  [the longest x1 10.1 us: graddrop(): return jnp.sum(keep * task_grads, axis=0)]
  transfers between devices with their start and end apart: 1 -> 0, of which waited for: 1 -> 0; matrix products, arithmetic and copies ran while one was open for 3% -> 0% of each run, Pallas kernels for 0% -> 0%
where the time goes in v1:
time: 198 us
  Pallas kernels  197 us (99%)
    pallas_call x1, Pallas kernels, run_block(): pl.pallas_call(functools.partial(block_kernel, plan), out_shape=(shape((c...  181 us
    pallas_call x1, Pallas kernels, widen(): pl.pallas_call(functools.partial(widen_kernel, plan), out_shape=(shape(he...  15.8 us

profile of v1, /device:TPU:0, one launch (start us, length us, event | category | flops | bytes accessed | tf_op | source)
XLA Modules:
  0.0 197.9 jit_solution(12103949433537154434)
XLA Ops:
  0.6 181.4 %block.1 = (bf16[576,768]{1,0:T(8,128)(2,1)}, bf16[576,2048]{1,0:T(8,128)(2,1)}, bf16[2,2,11776,128]{3,2,1,0:T(8,128)(2,1)}, f32[4,128]{1,0:T(4,128)}, f32[4,128...) custom-call(bf16[576,2048]{1,0:T(8,128)(2,1)} %bitcast.30, ...), custom_call_target="tpu_custom_call" | custom-call | tf_op jit(solution)/shard_map/block/pallas_call | solution.py:904
  182.1 15.8 %widen.1 = (bf16[576,768]{1,0:T(8,128)(2,1)}, bf16[576,2048]{1,0:T(8,128)(2,1)}, f32[2048,512]{1,0:T(8,128)}, f32[4608,512]{1,0:T(8,128)}, f32[512,2048]{1,0:T(8...) custom-call(bf16[2,2,11776,128]{3,2,1,0:T(8,128)(2,1)} %get-tuple-el, ...), custom_call_target="tpu_custom_call" | custom-call | tf_op jit(solution)/shard_map/widen/pallas_call | solution.py:994

commit v2 on v1

--- a/solution.py
+++ b/solution.py
@@ -15,7 +15,53 @@
 LOW = jnp.bfloat16
 NT = (((1,), (1,)), ((), ()))
 TN = (((0,), (0,)), ((), ()))
-SEGMENTS = ("heads", "expand", "spatial", "reduce")
+HEADS, EXPAND, SPATIAL, REDUCE = range(4)
+PARTS = (4, 2, 6, 4)
+ROUTES = (3, 0, 0, 0, 0, 4, 0, 5, 0, 0, 0, 3, 0, 3, 5, 0)
+(
+    AFTER_HEADS,
+    AFTER_THIRD,
+    AFTER_BACK_B,
+    AFTER_EXPAND,
+    AFTER_BACK_A,
+    AFTER_FIRST,
+    AFTER_REDUCE,
+    AFTER_SPATIAL,
+    AFTER_HALF,
+    LAST,
+) = range(100, 110)
+AGENDA = {
+    0: (0,),
+    1: (10,),
+    2: (20,),
+    3: (30,),
+    AFTER_THIRD: (1,),
+    AFTER_BACK_B: (11, 21,),
+    4: (40,),
+    5: (50, 31,),
+    AFTER_EXPAND: (2,),
+    AFTER_BACK_A: (22, 41, 12,),
+    6: (60, 32, 3,),
+    7: (70, 51,),
+    8: (80,),
+    9: (90, 42, 23, 13,),
+    AFTER_FIRST: (33,),
+    12: (120, 4, 61,),
+    13: (130, 52,),
+    14: (140,),
+    15: (150, 81, 71,),
+    10: (100, 43, 91,),
+    11: (110, 121, 34, 5,),
+    AFTER_SPATIAL: (24, 14, 62,),
+    AFTER_HALF: (131,),
+    LAST: (
+        44, 82, 72, 35, 53, 101, 151, 25, 63, 15, 92, 141, 132, 111, 83, 45, 122, 6, 36, 73, 54, 26, 102, 64,
+        152, 16, 142, 133, 93, 37, 55, 112, 27, 84, 17, 143, 46, 123, 38, 113, 7, 74, 103, 28, 65, 153, 134, 18,
+        94, 47, 56, 85, 144, 124, 8, 114, 75, 104, 66, 154, 135, 48, 95, 86, 57, 145, 125, 76, 115, 105, 67, 155,
+        136, 96, 87, 146, 77, 116, 68, 97, 58, 126, 106, 88, 156, 147, 137, 98, 127, 107, 157, 78, 138, 128, 117, 108,
+        148, 158, 118,
+    ),
+}
 
 
 class Plan:
@@ -35,20 +81,35 @@
         self.rows = self.count * self.step - self.height
         self.both = 2 * self.count * self.step - self.height
         self.half = self.wide // 2
-        unit = self.tasks * self.line * 16
-        real = {
-            "heads": self.heads // 256 * self.half,
-            "expand": self.half // 256 * self.mid,
-            "spatial": 9 * self.mid,
-            "reduce": self.mid // 256 * self.half,
-        }
-        self.real = real
-        self.size = {k: -(-real[k] // unit) * unit for k in SEGMENTS}
-        self.base, at = {}, 0
-        for k in SEGMENTS:
-            self.base[k] = at
-            at += self.size[k]
+        assert self.line & (self.line - 1) == 0
+        self.levels = self.line.bit_length() - 1
+        self.steps = 2 + self.levels
+        unit = 16 << self.steps
+        self.real = (
+            self.heads // 256 * self.half,
+            self.half // 256 * self.mid,
+            9 * self.mid,
+            self.mid // 256 * self.half,
+        )
+        tuned = self.steps == 4 and all(real % (n * unit) == 0 for real, n in zip(self.real, PARTS))
+        self.parts = PARTS if tuned else (1, 1, 1, 1)
+        self.base, self.first, self.segments, at = [], [], [], 0
+        for real, n in zip(self.real, self.parts):
+            self.base.append(at)
+            self.first.append(len(self.segments))
+            size = -(-real // (n * unit)) * unit
+            for _ in range(n):
+                index = len(self.segments)
+                self.segments.append((index, at, size, ROUTES[index] if tuned else 0))
+                at += size
         self.total = at
+        self.agenda = AGENDA
+        if not tuned:
+            self.stride = 2 * self.steps + 1
+            self.agenda = {i: (self.stride * i,) for i in range(4)}
+            self.agenda[LAST] = [self.stride * i + k for k in range(1, self.stride) for i in range(4)]
+        else:
+            self.stride = 10
 
 
 def chunk_of(rows):
@@ -141,13 +202,13 @@
         coef,
         msg,
         slots,
+        count_msg,
+        count_slots,
         wide_msg,
         wide_slots,
         total,
         terms,
-        recv_one,
-        recv_two,
-        recv_three,
+        received,
         load_sem,
         out_sem,
         sum_send,
@@ -156,7 +217,6 @@
         sib_recv,
         ring_send,
         ring_recv,
-        keep_sem,
     ) = scratch
     p = plan
     n_img, height, image, step = p.count, p.height, p.image, p.step
@@ -167,7 +227,11 @@
     core = lax.rem(dp, 2)
     level = dp // 2
     me = task * p.dp + dp
-    sibling = {"task": task, "dp": dp + 1 - 2 * core}
+
+    def place(at_task, at_dp):
+        return {"task": at_task, "dp": at_dp}
+
+    sibling = place(task, dp + 1 - 2 * core)
 
     def remote(src, dst, send, recv, device):
         return pltpu.make_async_remote_copy(
@@ -184,11 +248,9 @@
         pl.semaphore_signal(
             barrier,
             inc=1,
-            device_id={"task": other // p.dp, "dp": lax.rem(other, p.dp)},
+            device_id=place(other // p.dp, lax.rem(other, p.dp)),
             device_id_type=MESH,
         )
-
-    repeat(p.devices - 1, greet)
 
     loads = {
         "images": (images, img),
@@ -199,8 +261,15 @@
         "expand": (w_expand, we),
     }
     order = list(loads)
-    for i, key in enumerate(order):
-        pltpu.make_async_copy(*loads[key], load_sem.at[i]).start()
+
+    def load(key):
+        pltpu.make_async_copy(*loads[key], load_sem.at[order.index(key)]).start()
+
+    load("images")
+    load("reduce")
+    repeat(p.devices - 1, greet)
+    for key in order[2:]:
+        load(key)
     for row_tap in range(3):
         for col_tap in range(3):
             pltpu.make_async_copy(
@@ -224,25 +293,25 @@
         low_b[pl.ds(k * step, height)] = zero_rows
     low_b_all[pl.ds(rows, height)] = jnp.zeros((height, mid // 2), LOW)
 
+    def to_all(k, src, dst):
+        def send(i):
+            other = lax.rem(me + 1 + i, p.devices)
+            device = place(other // p.dp, lax.rem(other, p.dp))
+            remote(src, dst.at[me], sum_send.at[k], sum_recv.at[k], device).start()
+
+        repeat(p.devices - 1, send)
+
+    def from_all(k, dst):
+        some = dst.at[pl.ds(0, p.devices - 1)]
+        take(some, sum_recv.at[k])
+        take(some, sum_send.at[k])
+
     def sum_start(k, slot):
         slots[slot, me] = msg[k]
-
-        def send(i):
-            other = lax.rem(me + 1 + i, p.devices)
-            remote(
-                msg.at[k],
-                slots.at[slot, me],
-                sum_send.at[k],
-                sum_recv.at[k],
-                {"task": other // p.dp, "dp": lax.rem(other, p.dp)},
-            ).start()
-
-        repeat(p.devices - 1, send)
+        to_all(k, msg.at[k], slots.at[slot])
 
     def sum_finish(k, slot):
-        some = slots.at[slot, pl.ds(0, p.devices - 1)]
-        take(some, sum_recv.at[k])
-        take(some, sum_send.at[k])
+        from_all(k, slots.at[slot])
         total[pl.ds(0, 2 * mid_blocks)] = jnp.sum(slots[slot], axis=0)
 
     plane = 2 * p.tasks
@@ -257,7 +326,7 @@
                 wide_slots.at[k, spot],
                 sum_send.at[5 + 2 * k],
                 sum_recv.at[5 + 2 * k],
-                {"task": other // 2, "dp": level * 2 + lax.rem(other, 2)},
+                place(other // 2, level * 2 + lax.rem(other, 2)),
             ).start()
 
     def wide_turn(k):
@@ -274,7 +343,7 @@
                 wide_slots.at[k, plane + level],
                 sum_send.at[6 + 2 * k],
                 sum_recv.at[6 + 2 * k],
-                {"task": task, "dp": other * 2 + core},
+                place(task, other * 2 + core),
             ).start()
 
     def wide_finish(k):
@@ -284,161 +353,123 @@
         total[...] = jnp.sum(wide_slots[k, pl.ds(plane, p.line)], axis=0)
 
     low_bit, high_bit = lax.rem(task, 2), task // 2
-    near = {"task": task + 1 - 2 * low_bit, "dp": dp}
-    far = {"task": task + 2 - 4 * high_bit, "dp": dp}
-    routes = ((low_bit, high_bit, near, far), (high_bit, low_bit, far, near))
-
-    def ring(name, stage_at, part):
-        s = SEGMENTS.index(name)
-        return ring_send.at[s, stage_at, part], ring_recv.at[s, stage_at, part]
-
-    def put(name, row, values):
+    along_x = (low_bit, place(task + 1 - 2 * low_bit, dp))
+    along_y = (high_bit, place(task + 2 - 4 * high_bit, dp))
+    along_z = []
+    for k in range(p.levels):
+        bit = lax.rem(level // 2**k, 2)
+        along_z.append((bit, place(task, dp + 2 ** (k + 1) - 2 ** (k + 2) * bit)))
+
+    def route(kind, part):
+        one, two = (along_x, along_y) if part == 0 else (along_y, along_x)
+        return (
+            [one, two, *along_z],
+            [one, *along_z, two],
+            [*along_z, one, two],
+            [one, *along_z[:1], two, *along_z[1:]],
+            [*along_z[:1], one, *along_z[1:], two],
+            [*along_z[:1], one, two, *along_z[1:]],
+        )[kind]
+
+    def held(segment, part, k):
+        _, at, size, kind = segment
+        for j, (bit, _) in enumerate(route(kind, part)[:k]):
+            at = at + bit * (size >> (j + 1))
+        return at
+
+    def inbox(segment, k):
+        _, at, size, _ = segment
+        return at + size - (size >> k)
+
+    def put(family, row, values):
         low = values.astype(LOW)
-        at = span16(p.base[name] + row, low.shape[0])
+        at = span16(p.base[family] + row, low.shape[0])
         terms[0, at, :] = low[:, :128]
         terms[1, at, :] = low[:, 128:]
 
-    def add(part, to, others, count):
-        size = chunk_of(count)
+    def add_received(segment, part, at, rows_here, k):
+        starts = [inbox(segment, j) + at - held(segment, part, j + 1) for j in range(k)]
+        size = chunk_of(rows_here)
 
         def one(i):
-            at = span16(to + i * size, size)
-            acc = terms[part, at, :].astype(F32)
-            for read in others:
-                acc = acc + read(i * size, size)
-            terms[part, at, :] = acc.astype(LOW)
-
-        repeat(count // size, one)
-
-    def from_one(name, part, start):
-        return lambda i, size: recv_one[part, span16(p.base[name] // 2 + start + i, size), :].astype(F32)
-
-    def from_two(name, part):
-        return lambda i, size: recv_two[part, span16(p.base[name] // 4 + i, size), :].astype(F32)
-
-    def from_three(name, part, k):
-        return lambda i, size: recv_three[
-            part, k, span16(p.base[name] // (4 * p.line) + i, size), :
-        ].astype(F32)
-
-    def send_one(name):
-        size = p.size[name] // 2
-        for part, (mine, _, partner, _) in enumerate(routes):
-            send, recv = ring(name, 0, part)
+            here = span16(at + i * size, size)
+            acc = terms[part, here, :].astype(F32)
+            for start in starts:
+                acc = acc + received[part, span16(start + i * size, size), :].astype(F32)
+            terms[part, here, :] = acc.astype(LOW)
+
+        repeat(rows_here // size, one)
+
+    def some_of(segment, rows_here):
+        return received.at[:, pl.ds(segment[1], rows_here)]
+
+    def settle(segment, k, arrived, sent):
+        take(some_of(segment, arrived), ring_recv.at[segment[0], k])
+        take(some_of(segment, sent), ring_send.at[segment[0], 0])
+
+    def ring(segment, k):
+        return ring_send.at[segment[0], 0], ring_recv.at[segment[0], k]
+
+    def beside(segment):
+        return ring_send.at[segment[0], 1], ring_recv.at[segment[0], 2 * p.steps]
+
+    def home(part, start, rows_here):
+        return gathered.at[core, part, span16(start, rows_here)]
+
+    def scatter(segment, k):
+        _, _, size, kind = segment
+        here = size >> (k + 1)
+        if k:
+            settle(segment, k - 1, 2 * here, 2 * here)
+        for part in range(2):
+            bit, partner = route(kind, part)[k]
+            at = held(segment, part, k) + (1 - bit) * here
+            if k:
+                add_received(segment, part, at, here, k)
             remote(
-                terms.at[part, span16(p.base[name] + (1 - mine) * size, size)],
-                recv_one.at[part, pl.ds(p.base[name] // 2, size)],
-                send,
-                recv,
+                terms.at[part, span16(at, here)],
+                received.at[part, pl.ds(inbox(segment, k), here)],
+                *ring(segment, k),
                 partner,
             ).start()
 
-    def send_two(name):
-        size = p.size[name] // 4
-        for part, (mine, then, _, partner) in enumerate(routes):
-            send, recv = ring(name, 0, part)
-            some = recv_one.at[part, pl.ds(p.base[name] // 2, 2 * size)]
-            take(some, recv)
-            take(some, send)
-            at = p.base[name] + mine * 2 * size + (1 - then) * size
-            add(part, at, [from_one(name, part, (1 - then) * size)], size)
-            send, recv = ring(name, 1, part)
-            remote(
-                terms.at[part, span16(at, size)],
-                recv_two.at[part, pl.ds(p.base[name] // 4, size)],
-                send,
-                recv,
-                partner,
-            ).start()
-
-    def quarter(name, part):
-        mine, then, _, _ = routes[part]
-        return p.base[name] + (mine * 2 + then) * (p.size[name] // 4)
-
-    def send_three(name):
-        size = p.size[name] // 4
-        piece = size // p.line
-        for part, (mine, then, _, _) in enumerate(routes):
-            send, recv = ring(name, 1, part)
-            some = recv_two.at[part, pl.ds(p.base[name] // 4, size)]
-            take(some, recv)
-            take(some, send)
-            at = quarter(name, part)
-            add(part, at, [from_one(name, part, then * size), from_two(name, part)], size)
-            send, recv = ring(name, 2, part)
-            for i in range(1, p.line):
-                other = lax.rem(level + i, p.line)
-                remote(
-                    terms.at[part, span16(at + other * piece, piece)],
-                    recv_three.at[part, i - 1, pl.ds(p.base[name] // (4 * p.line), piece)],
-                    send,
-                    recv,
-                    {"task": task, "dp": other * 2 + core},
-                ).start()
-
-    def home(name, part, start, size):
-        return gathered.at[core, part, span16(start, size)]
-
-    def gather_one(name):
-        s = SEGMENTS.index(name)
-        piece = p.size[name] // 4 // p.line
+    def gather(segment, k):
+        _, _, size, kind = segment
+        here = size >> (k + 1)
+        if k == p.steps - 1:
+            settle(segment, k, here, here)
+        else:
+            settle(segment, p.steps + k + 1, here // 2, here if k == p.steps - 2 else here // 2)
         for part in range(2):
-            send, recv = ring(name, 2, part)
-            some = recv_three.at[part, pl.ds(0, p.line - 1), pl.ds(p.base[name] // (4 * p.line), piece)]
-            take(some, recv)
-            take(some, send)
-            at = quarter(name, part) + level * piece
-            add(part, at, [from_three(name, part, k) for k in range(p.line - 1)], piece)
-            send, recv = ring(name, 3, part)
-            mine = terms.at[part, span16(at, piece)]
-            for i in range(1, p.line):
-                other = lax.rem(level + i, p.line)
-                target = {"task": task, "dp": other * 2 + core}
-                remote(mine, home(name, part, at, piece), send, recv, target).start()
-            pltpu.make_async_copy(mine, home(name, part, at, piece), keep_sem.at[s, part]).start()
-
-    def gather_two(name):
-        s = SEGMENTS.index(name)
-        size = p.size[name] // 4
-        piece = size // p.line
-        for part, (_, _, _, partner) in enumerate(routes):
-            send, recv = ring(name, 3, part)
-            some = recv_three.at[part, pl.ds(0, p.line - 1), pl.ds(p.base[name] // (4 * p.line), piece)]
-            take(some, recv)
-            take(some, send)
-            at = quarter(name, part)
-            take(terms.at[part, span16(at, piece)], keep_sem.at[s, part])
-            mine = home(name, part, at, size)
-            send, recv = ring(name, 4, part)
-            remote(mine, mine, send, recv, partner).start()
-
-    def gather_three(name):
-        size = p.size[name] // 2
-        for part, (mine, _, partner, _) in enumerate(routes):
-            send, recv = ring(name, 4, part)
-            some = recv_two.at[part, pl.ds(p.base[name] // 4, size // 2)]
-            take(some, recv)
-            take(some, send)
-            ours = home(name, part, p.base[name] + mine * size, size)
-            send, recv = ring(name, 5, part)
-            remote(ours, ours, send, recv, partner).start()
-
-    def gather_four(name):
+            partner = route(kind, part)[k][1]
+            at = held(segment, part, k + 1)
+            mine = ours = home(part, at, here)
+            if k == p.steps - 1:
+                add_received(segment, part, at, here, p.steps)
+                mine = terms.at[part, span16(at, here)]
+                pltpu.make_async_copy(mine, ours, ring_send.at[segment[0], 0]).start()
+            remote(mine, ours, *ring(segment, p.steps + k), partner).start()
+            if k == 0:
+                remote(ours, ours, *beside(segment), sibling).start()
+
+    def share(segment):
+        _, at, size, kind = segment
+        settle(segment, p.steps, size // 2, size // 2)
+        take(some_of(segment, size // 2), ring_send.at[segment[0], 1])
         for part in range(2):
-            send, recv = ring(name, 5, part)
-            some = recv_one.at[part, pl.ds(p.base[name] // 2, p.size[name] // 2)]
-            take(some, recv)
-            take(some, send)
-            send, recv = ring(name, 6, part)
-            ours = home(name, part, p.base[name], p.size[name])
-            remote(ours, ours, send, recv, sibling).start()
-
-    def gather_end(name):
-        for part in range(2):
-            send, recv = ring(name, 6, part)
-            some = terms.at[part, pl.ds(p.base[name], p.size[name])]
-            take(some, send)
-            take(some, recv)
+            bit = route(kind, part)[0][0]
+            ours = home(part, at + (1 - bit) * (size // 2), size // 2)
+            remote(ours, ours, *beside(segment), sibling).start()
+
+    def travel(point):
+        for todo in p.agenda.get(point, ()):
+            segment, k = p.segments[todo // p.stride], todo % p.stride
+            if k < p.steps:
+                scatter(segment, k)
+            elif k < 2 * p.steps:
+                gather(segment, 2 * p.steps - 1 - k)
+            else:
+                share(segment)
 
     other_half = pl.ds(pl.multiple_of((1 - core) * half, 128), half)
     other_quarter = pl.ds(pl.multiple_of(mid + (1 - core) * (mid // 2), 128), mid // 2)
@@ -457,16 +488,12 @@
         src, dst = swaps[k]
         return remote(src, dst, sib_send.at[k], sib_recv.at[k], sibling)
 
-    msg[0] = jnp.broadcast_to(fold(column_sum(mask[...])), (2 * mid_blocks, 128))
-    pl.semaphore_wait(barrier, p.devices - 1)
-    sum_start(0, 0)
-    swap(0).start()
-    swap(1).start()
-
     def put_stats(ref, at, blocks, block, one, two):
         ref[(*at, pl.ds(block, 1))] = fold(one)
         ref[(*at, pl.ds(blocks + block, 1))] = fold(two)
 
+    count_msg[...] = fold(column_sum(mask[...]))
+    count_slots[me] = count_msg[...]
     loaded("images")
     loaded("reduce")
 
@@ -484,9 +511,6 @@
             put_stats(msg, (1,), mid_blocks, 2 * nb + h, one, two)
 
     repeat(mid // 256, first_layer)
-    sum_finish(0, 0)
-    count = total[pl.ds(0, 1)]
-    sum_start(1, 1)
 
     loaded("grad")
     loaded("heads")
@@ -518,8 +542,19 @@
 
         repeat(cells // 64, drop)
 
-    repeat(wide // 256, merge)
-    swap(0).wait_recv()
+    blocks = wide // 256
+    cuts = [0, blocks // 4, blocks * 5 // 8, blocks * 6 // 8, blocks]
+
+    def merge_some(k):
+        lax.fori_loop(cuts[k], cuts[k + 1], lambda i, carry: (merge(i), carry)[1], 0)
+
+    merge_some(0)
+    pl.semaphore_wait(barrier, p.devices - 1)
+    to_all(0, count_msg, count_slots)
+    sum_start(1, 1)
+    swap(0).start()
+    swap(1).start()
+    merge_some(1)
 
     def turn_images(j):
         own = img[:, pl.ds(pl.multiple_of(core * half + j * 128, 128), 128)]
@@ -546,6 +581,8 @@
         for h, part in enumerate((up, values, down)):
             ref[at, pl.ds(pl.multiple_of(h * mid + block * 128, 128), 128)] = part.astype(LOW)
 
+    from_all(0, count_slots)
+    count = jnp.sum(count_slots[...], axis=0)
     sum_finish(1, 1)
     center(mid_blocks)
     coef[2, pl.ds(0, mid_blocks)] = coef[1, pl.ds(0, mid_blocks)]
@@ -580,6 +617,8 @@
 
     repeat(mid // 256, second_layer)
     sum_start(2, 0)
+    merge_some(2)
+    swap(0).wait_recv()
     repeat(half // 128, turn_images)
     sum_finish(2, 0)
     center(mid_blocks)
@@ -611,6 +650,7 @@
 
     repeat(wide // 256, third_layer)
     wide_start(0)
+    merge_some(3)
     swap(3).wait_recv()
     wide_turn(0)
 
@@ -623,7 +663,8 @@
 
     chunk = chunk_of(image)
 
-    def normalize_c(cb):
+    def normalize_c(i):
+        cb = lax.rem(i + (1 - core) * (wide_blocks // 2), wide_blocks)
         gain, shift = gain_c[pl.ds(cb, 1)], shift_c[pl.ds(cb, 1)]
         one = two = jnp.zeros((8, 128), F32)
         for k in range(n_img):
@@ -641,17 +682,14 @@
                 two = two + column_sum(up * hat)
         put_stats(wide_msg, (1, 0), wide_blocks, cb, one, two)
 
-    repeat(wide_blocks, normalize_c)
+    def both_halves(body, k):
+        repeat(wide_blocks // 2, body)
+        swap(k).start()
+        repeat(wide_blocks // 2, lambda i: body(i + wide_blocks // 2))
+
+    both_halves(normalize_c, 4)
     wide_start(1)
-    swap(4).start()
-
-    def head_layer(nb):
-        values = jnp.dot(trunk[...], wh[:, lanes(nb, 256)], preferred_element_type=F32)
-        stage[:, lanes(nb, 256)] = values.astype(LOW)
-
-    repeat(p.heads // 256, head_layer)
-    pltpu.make_async_copy(stage, head_out, out_sem.at[0]).start()
-    wide_turn(1)
+
     swap(1).wait_recv()
     swap(4).wait_recv()
 
@@ -660,10 +698,25 @@
         both = jnp.concatenate([own, sib_two[:, lanes(j, 256)]], axis=0)
         values = lax.dot_general(both, hg[...], TN, preferred_element_type=F32)
         for b in range(p.heads // 256):
-            put("heads", b * half + j * 256, values[:, b * 256 : b * 256 + 256])
-
-    repeat(half // 256, heads_gradient)
-    send_one("heads")
+            put(HEADS, j * p.heads + b * 256, values[:, b * 256 : b * 256 + 256])
+
+    def each(family, total, body):
+        n = p.parts[family]
+        per = total // n
+        for i in range(n):
+            repeat(per, lambda j, i=i: body(i * per + j))
+            travel(p.first[family] + i)
+
+    each(HEADS, half // 256, heads_gradient)
+    wide_turn(1)
+
+    def head_layer(nb):
+        values = jnp.dot(trunk[...], wh[:, lanes(nb, 256)], preferred_element_type=F32)
+        stage[:, lanes(nb, 256)] = values.astype(LOW)
+
+    repeat(p.heads // 256, head_layer)
+    pltpu.make_async_copy(stage, head_out, out_sem.at[0]).start()
+    travel(AFTER_HEADS)
     swap(4).wait_send()
     wide_finish(1)
 
@@ -677,7 +730,8 @@
     gain_c_grad[...] = total[pl.ds(wide_blocks, wide_blocks)]
     backward(wide_blocks, gain_c[...], coef[1])
 
-    def third_gradient(cb):
+    def third_gradient(i):
+        cb = lax.rem(i + (1 - core) * (wide_blocks // 2), wide_blocks)
         for k in range(n_img):
             for r in range(image // chunk):
                 at = pl.ds(k * image + r * chunk, chunk)
@@ -685,8 +739,8 @@
                 down = merged[at, lanes(cb)] * row(4, cb) + row(5, cb) + third[at, lanes(cb)] * row(6, cb)
                 trunk[at, lanes(cb)] = (down * valid).astype(LOW)
 
-    repeat(wide_blocks, third_gradient)
-    swap(5).start()
+    both_halves(third_gradient, 5)
+    travel(AFTER_THIRD)
 
     def slope_of(pre):
         gate = logistic(pre)
@@ -710,16 +764,16 @@
 
     repeat(mid // 256, third_back)
     sum_start(3, 1)
-    send_two("heads")
+    travel(AFTER_BACK_B)
     swap(5).wait_recv()
 
     def expand_gradient(j):
         own = trunk[:, pl.ds(pl.multiple_of(core * half + j * 256, 128), 256)]
         both = jnp.concatenate([own, sib_one[:, lanes(j, 256)]], axis=0)
-        put("expand", j * mid, jnp.dot(hid_b_t[...], both, preferred_element_type=F32))
-
-    repeat(half // 256, expand_gradient)
-    send_one("expand")
+        put(EXPAND, j * mid, jnp.dot(hid_b_t[...], both, preferred_element_type=F32))
+
+    each(EXPAND, half // 256, expand_gradient)
+    travel(AFTER_EXPAND)
     sum_finish(3, 1)
     shift_b_grad[...] = total[pl.ds(0, mid_blocks)]
     gain_b_grad[...] = total[pl.ds(mid_blocks, mid_blocks)]
@@ -765,25 +819,30 @@
 
     repeat(mid // 256, second_back)
     sum_start(4, 0)
-    send_three("heads")
-    send_two("expand")
+    travel(AFTER_BACK_A)
     swap(2).wait_recv()
     swap(6).wait_recv()
+    per_tap = 3 * mid // 256
 
     def spatial_gradient(i):
-        per = 3 * mid // 256
-        j, k = i // per, lax.rem(i, per)
-        row_tap, sub = k // (mid // 256), lax.rem(k, mid // 256)
+        j, k = i // per_tap, lax.rem(i, per_tap)
         values = lax.dot_general(
             hid_a[span16(j * height, p.both), lanes(k, 256)],
             low_b_all[...],
             TN,
             preferred_element_type=F32,
         )
-        put("spatial", (row_tap * 3 + j) * mid + sub * 256, values)
-
-    repeat(9 * mid // 256, spatial_gradient)
-    send_one("spatial")
+        put(SPATIAL, i * 256, values)
+
+    def spatial_some(first_part, last_part):
+        n = p.parts[SPATIAL]
+        per = 3 * per_tap // n
+        for i in range(first_part, last_part):
+            repeat(per, lambda j, i=i: spatial_gradient(i * per + j))
+            travel(p.first[SPATIAL] + i)
+
+    early = p.parts[SPATIAL] * 2 // 3
+    spatial_some(0, early)
     sum_finish(4, 0)
     shift_a_grad[...] = total[pl.ds(0, mid_blocks)]
     gain_a_grad[...] = total[pl.ds(mid_blocks, mid_blocks)]
@@ -797,18 +856,20 @@
 
     repeat(mid_blocks, first_gradient)
     swap(7).start()
-    gather_one("heads")
-    send_three("expand")
+    travel(AFTER_FIRST)
     swap(7).wait_recv()
 
-    def reduce_gradient(i):
-        j, b = i // (mid // 256), lax.rem(i, mid // 256)
-        values = jnp.dot(img_t[lanes(j, 256), :], low_a[:, lanes(b, 256)], preferred_element_type=F32)
-        put("reduce", b * half + j * 256, values)
-
-    repeat(half // 256 * (mid // 256), reduce_gradient)
-    send_one("reduce")
-    send_two("spatial")
+    def reduce_gradient(j):
+        def one(b):
+            values = jnp.dot(img_t[lanes(j, 256), :], low_a[:, lanes(b, 256)], preferred_element_type=F32)
+            put(REDUCE, j * mid + b * 256, values)
+
+        repeat(mid // 256, one)
+
+    each(REDUCE, half // 256, reduce_gradient)
+    travel(AFTER_REDUCE)
+    spatial_some(early, p.parts[SPATIAL])
+    travel(AFTER_SPATIAL)
 
     def first_back(nb):
         values = lax.dot_general(low_a[pl.ds(0, cells)], wr[lanes(nb, 256), :], NT, preferred_element_type=F32)
@@ -819,29 +880,16 @@
                 part = (part + merged[at, lanes(2 * nb + h)]) * mask[pl.ds(k * step, image)]
                 img[at, lanes(2 * nb + h)] = part.astype(LOW)
 
-    repeat(wide // 256, first_back)
+    repeat(wide // 512, first_back)
+    travel(AFTER_HALF)
+    repeat(wide // 512, lambda i: first_back(i + wide // 512))
     pltpu.make_async_copy(img, grad_images, out_sem.at[1]).start()
 
-    gather_two("heads")
-    gather_one("expand")
-    send_two("reduce")
-    gather_three("heads")
-    gather_two("expand")
-    send_three("spatial")
-    gather_four("heads")
-    send_three("reduce")
-    gather_three("expand")
-    gather_one("spatial")
-    gather_four("expand")
-    gather_one("reduce")
-    gather_two("spatial")
-    gather_two("reduce")
-    gather_three("spatial")
-    gather_three("reduce")
-    gather_four("spatial")
-    gather_four("reduce")
-    for name in SEGMENTS:
-        gather_end(name)
+    travel(LAST)
+    for segment in p.segments:
+        send, recv = beside(segment)
+        take(some_of(segment, segment[2]), recv)
+        take(some_of(segment, segment[2] // 2), send)
     pltpu.make_async_copy(stage, head_out, out_sem.at[0]).wait()
     pltpu.make_async_copy(img, grad_images, out_sem.at[1]).wait()
     for k in (0, 1, 2, 3, 5, 6, 7):
@@ -884,22 +932,21 @@
         pltpu.VMEM((7, wide_blocks, 128), F32),
         pltpu.VMEM((5, 2 * mid_blocks, 128), F32),
         pltpu.VMEM((2, p.devices, 2 * mid_blocks, 128), F32),
+        pltpu.VMEM((1, 128), F32),
+        pltpu.VMEM((p.devices, 1, 128), F32),
         pltpu.VMEM((2, 2, 2 * wide_blocks, 128), F32),
         pltpu.VMEM((2, 2 * p.tasks + p.line, 2 * wide_blocks, 128), F32),
         pltpu.VMEM((2 * wide_blocks, 128), F32),
         pltpu.VMEM((2, p.total, 128), LOW),
-        pltpu.VMEM((2, p.total // 2, 128), LOW),
-        pltpu.VMEM((2, p.total // 4, 128), LOW),
-        pltpu.VMEM((2, p.line - 1, p.total // (4 * p.line), 128), LOW),
+        pltpu.VMEM((2, p.total, 128), LOW),
         pltpu.SemaphoreType.DMA((7,)),
         pltpu.SemaphoreType.DMA((2,)),
         pltpu.SemaphoreType.DMA((9,)),
         pltpu.SemaphoreType.DMA((9,)),
         pltpu.SemaphoreType.DMA((8,)),
         pltpu.SemaphoreType.DMA((8,)),
-        pltpu.SemaphoreType.DMA((4, 7, 2)),
-        pltpu.SemaphoreType.DMA((4, 7, 2)),
-        pltpu.SemaphoreType.DMA((4, 2)),
+        pltpu.SemaphoreType.DMA((len(p.segments), 2)),
+        pltpu.SemaphoreType.DMA((len(p.segments), 2 * p.steps + 1)),
     ]
     return pl.pallas_call(
         functools.partial(block_kernel, plan),
@@ -942,9 +989,9 @@
     for one in fetches:
         one.start()
     loads = []
-    for s, name in enumerate(SEGMENTS):
+    for s in range(4):
         for core in range(2):
-            at = (core, slice(None), pl.ds(p.base[name], p.real[name]))
+            at = (core, slice(None), pl.ds(p.base[s], p.real[s]))
             load = pltpu.make_async_copy(gathered.at[at], low.at[at], load_sem.at[s, core])
             load.start()
             loads.append(load)
@@ -953,25 +1000,32 @@
         one.start()
     for src, dst in zip(small_in, small_out):
         dst[...] = src[...]
-    where = {
-        "heads": (heads, out_heads, p.half, p.heads, True),
-        "expand": (expand, out_expand, p.mid, p.half, False),
-        "spatial": (spatial, out_spatial, 9 * p.mid, p.mid // 2, False),
-        "reduce": (reduce, out_reduce, p.half, p.mid, True),
-    }
+    where = (
+        (heads, out_heads, p.half, p.heads, True),
+        (expand, out_expand, p.mid, p.half, False),
+        (spatial, out_spatial, 9 * p.mid, p.mid // 2, False),
+        (reduce, out_reduce, p.half, p.mid, True),
+    )
     copies = []
-    for s, name in enumerate(SEGMENTS):
-        wide, out, height, width, by_rows = where[name]
+    per_tap = p.mid // 256
+    for s, (wide, out, height, width, by_rows) in enumerate(where):
         for core in range(2):
             loads[2 * s + core].wait()
             size = 256
             row_at = core * height if by_rows else 0
             col_at = 0 if by_rows else core * width
 
-            def one(i, name=name, wide=wide, out=out, row_at=row_at, col_at=col_at, s=s, core=core):
+            def one(i, s=s, wide=wide, out=out, row_at=row_at, col_at=col_at, core=core):
                 rows = pl.ds(pl.multiple_of(row_at + i * size, size), size)
                 for b in range(width // 256):
-                    src = pl.ds(pl.multiple_of(p.base[name] + b * height + i * size, size), size)
+                    if s == EXPAND:
+                        start = b * height + i * size
+                    elif s == SPATIAL:
+                        tap, sub = i // per_tap, lax.rem(i, per_tap)
+                        start = (lax.rem(tap, 3) * 3 + tap // 3) * p.mid + sub * size
+                    else:
+                        start = i * width + b * size
+                    src = pl.ds(pl.multiple_of(p.base[s] + start, size), size)
                     for part in range(2):
                         cols = pl.ds(col_at + b * 256 + part * 128, 128)
                         wide[rows, cols] = low[core, part, src, :].astype(F32)

time: 198 us -> 160 us (0.81)
  Pallas kernels: 197 us -> 159 us
    pallas_call x1, Pallas kernels: 181 us -> 143 us  [run_block(): pl.pallas_call(functools.partial(block_kernel, plan), out_shape=(shape((c...]
where the time goes in v2:
time: 160 us
  Pallas kernels  159 us (99%)
    pallas_call x1, Pallas kernels, run_block(): pl.pallas_call(functools.partial(block_kernel, plan), out_shape=(shape((c...  143 us
    pallas_call x1, Pallas kernels, widen(): pl.pallas_call(functools.partial(widen_kernel, plan), out_shape=(shape(he...  15.8 us

profile of v2, /device:TPU:0, one launch (start us, length us, event | category | flops | bytes accessed | tf_op | source)
XLA Modules:
  0.0 159.6 jit_solution(13817576615461706393)
XLA Ops:
  0.6 143.0 %block.1 = (bf16[576,768]{1,0:T(8,128)(2,1)}, bf16[576,2048]{1,0:T(8,128)(2,1)}, bf16[2,2,11776,128]{3,2,1,0:T(8,128)(2,1)}, f32[4,128]{1,0:T(4,128)}, f32[4,128...) custom-call(bf16[576,2048]{1,0:T(8,128)(2,1)} %bitcast.30, ...), custom_call_target="tpu_custom_call" | custom-call | tf_op jit(solution)/shard_map/block/pallas_call | solution.py:951
  143.7 15.8 %widen.1 = (bf16[576,768]{1,0:T(8,128)(2,1)}, bf16[576,2048]{1,0:T(8,128)(2,1)}, f32[2048,512]{1,0:T(8,128)}, f32[4608,512]{1,0:T(8,128)}, f32[512,2048]{1,0:T(8...) custom-call(bf16[2,2,11776,128]{3,2,1,0:T(8,128)(2,1)} %get-tuple-el, ...), custom_call_target="tpu_custom_call" | custom-call | tf_op jit(solution)/shard_map/widen/pallas_call | solution.py:1048

commit v3 on v2

--- a/solution.py
+++ b/solution.py
@@ -17,49 +17,55 @@
 TN = (((0,), (0,)), ((), ()))
 HEADS, EXPAND, SPATIAL, REDUCE = range(4)
 PARTS = (4, 2, 6, 4)
-ROUTES = (3, 0, 0, 0, 0, 4, 0, 5, 0, 0, 0, 3, 0, 3, 5, 0)
+ROUTES = (0, 0, 0, 0, 5, 0, 5, 0, 0, 0, 0, 3, 5, 4, 0, 3)
 (
-    AFTER_HEADS,
-    AFTER_THIRD,
-    AFTER_BACK_B,
-    AFTER_EXPAND,
-    AFTER_BACK_A,
+    AFTER_HEADS_0,
+    AFTER_HEADS_1,
+    AFTER_HEADS_2,
+    AFTER_THIRD_0,
+    AFTER_THIRD_1,
+    AFTER_BACK_B_1,
+    AFTER_EXPAND_END,
+    AFTER_SECOND,
+    AFTER_BACK_A_1,
     AFTER_FIRST,
-    AFTER_REDUCE,
-    AFTER_SPATIAL,
-    AFTER_HALF,
+    AFTER_REDUCE_END,
+    AFTER_SPATIAL_END,
+    AFTER_LAST_0,
+    AFTER_LAST_1,
+    AFTER_LAST_2,
     LAST,
-) = range(100, 110)
+) = range(100, 116)
 AGENDA = {
     0: (0,),
     1: (10,),
     2: (20,),
     3: (30,),
-    AFTER_THIRD: (1,),
-    AFTER_BACK_B: (11, 21,),
+    AFTER_THIRD_0: (1,),
+    AFTER_BACK_B_1: (11, 21,),
     4: (40,),
     5: (50, 31,),
-    AFTER_EXPAND: (2,),
-    AFTER_BACK_A: (22, 41, 12,),
-    6: (60, 32, 3,),
-    7: (70, 51,),
+    AFTER_EXPAND_END: (2, 12,),
+    AFTER_BACK_A_1: (22, 51, 32,),
+    6: (60, 41,),
+    7: (70, 3, 13,),
     8: (80,),
-    9: (90, 42, 23, 13,),
-    AFTER_FIRST: (33,),
-    12: (120, 4, 61,),
-    13: (130, 52,),
-    14: (140,),
-    15: (150, 81, 71,),
-    10: (100, 43, 91,),
-    11: (110, 121, 34, 5,),
-    AFTER_SPATIAL: (24, 14, 62,),
-    AFTER_HALF: (131,),
+    9: (90, 23, 52,),
+    10: (100, 33, 42,),
+    12: (120, 71,),
+    13: (130,),
+    14: (140, 61,),
+    15: (150, 4, 81,),
+    11: (110, 24, 14,),
+    AFTER_LAST_0: (91, 53,),
+    AFTER_LAST_1: (34,),
+    AFTER_LAST_2: (101,),
     LAST: (
-        44, 82, 72, 35, 53, 101, 151, 25, 63, 15, 92, 141, 132, 111, 83, 45, 122, 6, 36, 73, 54, 26, 102, 64,
-        152, 16, 142, 133, 93, 37, 55, 112, 27, 84, 17, 143, 46, 123, 38, 113, 7, 74, 103, 28, 65, 153, 134, 18,
-        94, 47, 56, 85, 144, 124, 8, 114, 75, 104, 66, 154, 135, 48, 95, 86, 57, 145, 125, 76, 115, 105, 67, 155,
-        136, 96, 87, 146, 77, 116, 68, 97, 58, 126, 106, 88, 156, 147, 137, 98, 127, 107, 157, 78, 138, 128, 117, 108,
-        148, 158, 118,
+        72, 43, 121, 141, 131, 62, 5, 25, 151, 15, 54, 82, 35, 73, 111, 44, 6, 92, 26, 102, 122, 152, 142, 16,
+        132, 63, 55, 7, 83, 27, 36, 123, 153, 74, 17, 112, 8, 45, 93, 103, 28, 143, 37, 133, 64, 56, 18, 113,
+        84, 124, 46, 154, 75, 94, 104, 38, 134, 144, 65, 114, 57, 85, 76, 135, 47, 125, 155, 66, 95, 105, 86, 145,
+        58, 115, 77, 126, 156, 136, 67, 87, 116, 48, 96, 78, 127, 106, 137, 146, 157, 88, 97, 107, 147, 68, 158, 117,
+        98, 108, 128, 148, 138, 118,
     ),
 }
 
@@ -71,16 +77,19 @@
         self.line = self.dp // 2
         self.devices = self.tasks * self.dp
         assert self.tasks == 4 and self.dp % 2 == 0
+        assert self.devices & (self.devices - 1) == 0
         self.count, self.height, self.span, self.wide = images.shape
         assert self.height & (self.height - 1) == 0 and self.height % 16 == 0
         self.mid = w_reduce.shape[1]
         self.heads = w_heads.shape[1]
+        assert self.mid == 512 and self.heads == 768 and self.wide == 2048
         self.image = self.height * self.span
         self.cells = self.count * self.image
         self.step = self.image + self.height
         self.rows = self.count * self.step - self.height
         self.both = 2 * self.count * self.step - self.height
         self.half = self.wide // 2
+        self.depth = -(-self.both // 256) * 256
         assert self.line & (self.line - 1) == 0
         self.levels = self.line.bit_length() - 1
         self.steps = 2 + self.levels
@@ -175,7 +184,6 @@
     *scratch,
 ):
     (
-        img,
         wr,
         ws,
         we,
@@ -195,9 +203,7 @@
         hid_b_t,
         low_b,
         low_b_all,
-        low_a,
         gsc,
-        stage,
         mask,
         coef,
         msg,
@@ -210,7 +216,6 @@
         terms,
         received,
         load_sem,
-        out_sem,
         sum_send,
         sum_recv,
         sib_send,
@@ -218,15 +223,18 @@
         ring_send,
         ring_recv,
     ) = scratch
+    img, stage, low_a = grad_images, head_out, hid_b
     p = plan
     n_img, height, image, step = p.count, p.height, p.image, p.step
     cells, rows, mid, wide, half = p.cells, p.rows, p.mid, p.wide, p.half
     mid_blocks, wide_blocks = mid // 128, wide // 128
+    chunk = chunk_of(image)
     task = lax.axis_index("task")
     dp = lax.axis_index("dp")
     core = lax.rem(dp, 2)
     level = dp // 2
     me = task * p.dp + dp
+    none = dp // p.dp
 
     def place(at_task, at_dp):
         return {"task": at_task, "dp": at_dp}
@@ -244,7 +252,7 @@
     barrier = pltpu.get_barrier_semaphore()
 
     def greet(i):
-        other = lax.rem(me + 1 + i, p.devices)
+        other = me ^ (p.devices - 1 - i)
         pl.semaphore_signal(
             barrier,
             inc=1,
@@ -289,13 +297,16 @@
     zero_rows = jnp.zeros((height, 3 * mid), LOW)
     for k in range(2 * n_img + 1):
         hid_a[pl.ds(k * step, height)] = zero_rows
+    beyond = p.depth - p.both
+    hid_a[pl.ds(p.both + 2 * height, beyond)] = jnp.zeros((beyond, 3 * mid), LOW)
+    low_b_all[pl.ds(p.both, beyond)] = jnp.zeros((beyond, mid // 2), LOW)
     for k in range(n_img + 1):
         low_b[pl.ds(k * step, height)] = zero_rows
     low_b_all[pl.ds(rows, height)] = jnp.zeros((height, mid // 2), LOW)
 
     def to_all(k, src, dst):
         def send(i):
-            other = lax.rem(me + 1 + i, p.devices)
+            other = me ^ (p.devices - 1 - i)
             device = place(other // p.dp, lax.rem(other, p.dp))
             remote(src, dst.at[me], sum_send.at[k], sum_recv.at[k], device).start()
 
@@ -319,8 +330,8 @@
 
     def wide_start(k):
         wide_slots[k, spot] = wide_msg[k, 0]
-        for i in range(1, plane):
-            other = lax.rem(spot + i, plane)
+        for i in range(plane - 1, 0, -1):
+            other = spot ^ i
             remote(
                 wide_msg.at[k, 0],
                 wide_slots.at[k, spot],
@@ -336,8 +347,8 @@
         partial = jnp.sum(wide_slots[k, pl.ds(0, plane)], axis=0)
         wide_msg[k, 1] = partial
         wide_slots[k, plane + level] = partial
-        for i in range(1, p.line):
-            other = lax.rem(level + i, p.line)
+        for i in range(p.line - 1, 0, -1):
+            other = level ^ i
             remote(
                 wide_msg.at[k, 1],
                 wide_slots.at[k, plane + level],
@@ -403,15 +414,17 @@
     def some_of(segment, rows_here):
         return received.at[:, pl.ds(segment[1], rows_here)]
 
+    def ring(segment, k):
+        at = k - p.steps - 1 if k > p.steps else k
+        return ring_send.at[segment[0], 0], ring_recv.at[segment[0], at]
+
     def settle(segment, k, arrived, sent):
-        take(some_of(segment, arrived), ring_recv.at[segment[0], k])
-        take(some_of(segment, sent), ring_send.at[segment[0], 0])
-
-    def ring(segment, k):
-        return ring_send.at[segment[0], 0], ring_recv.at[segment[0], k]
+        send, recv = ring(segment, k)
+        take(some_of(segment, arrived), recv)
+        take(some_of(segment, sent), send)
 
     def beside(segment):
-        return ring_send.at[segment[0], 1], ring_recv.at[segment[0], 2 * p.steps]
+        return ring_send.at[segment[0], 1], ring_recv.at[segment[0], p.steps + 1]
 
     def home(part, start, rows_here):
         return gathered.at[core, part, span16(start, rows_here)]
@@ -498,19 +511,19 @@
     loaded("reduce")
 
     def first_layer(nb):
-        values = jnp.dot(img[...], wr[:, lanes(nb, 256)], preferred_element_type=F32)
-        for h in range(2):
+        values = jnp.dot(img[...], wr[:, lanes(nb, 512)], preferred_element_type=F32)
+        for h in range(4):
             one = two = jnp.zeros((8, 128), F32)
             for k in range(n_img):
                 at = pl.ds(k * image, image)
                 part = values[k * image : (k + 1) * image, h * 128 : h * 128 + 128]
                 part = part * mask[pl.ds(k * step, image)]
-                first[at, lanes(2 * nb + h)] = part
+                first[at, lanes(4 * nb + h)] = part
                 one = one + column_sum(part)
                 two = two + column_sum(part * part)
-            put_stats(msg, (1,), mid_blocks, 2 * nb + h, one, two)
-
-    repeat(mid // 256, first_layer)
+            put_stats(msg, (1,), mid_blocks, 4 * nb + h, one, two)
+
+    first_layer(none)
 
     loaded("grad")
     loaded("heads")
@@ -527,7 +540,9 @@
             gsc[t] = values.astype(LOW)
 
         def drop(i):
-            at = span16(i * 64, 64)
+            at = span16(i * chunk, chunk)
+            per = image // chunk
+            valid = mask[span16(i // per * step + lax.rem(i, per) * chunk, chunk)]
             for h in range(2):
                 grads = [gsc[t, at, pl.ds(h * 128, 128)].astype(F32) for t in range(TASKS)]
                 signed, size, kept = 0.0, 0.0, 0.0
@@ -538,9 +553,9 @@
                     kept = kept + jnp.tanh(g * 5.0) * g
                 limit = trunk[at, lanes(2 * nb + h)].astype(F32)
                 lean = jnp.tanh(2.5 + 2.5 * (signed / size) - 5.0 * limit)
-                merged[at, lanes(2 * nb + h)] = 0.5 * (signed + lean * kept)
-
-        repeat(cells // 64, drop)
+                merged[at, lanes(2 * nb + h)] = (0.25 * valid) * (signed + lean * kept)
+
+        repeat(cells // chunk, drop)
 
     blocks = wide // 256
     cuts = [0, blocks // 4, blocks * 5 // 8, blocks * 6 // 8, blocks]
@@ -607,15 +622,15 @@
         values = None
         for j in range(3):
             term = jnp.dot(
-                hid_a[pl.ds(j * height, rows)], ws[j, :, lanes(nb, 256)], preferred_element_type=F32
+                hid_a[pl.ds(j * height, rows)], ws[j, :, lanes(nb, 512)], preferred_element_type=F32
             )
             values = term if values is None else values + term
-        for h in range(2):
+        for h in range(4):
             part = values[:, h * 128 : h * 128 + 128] * mask[...]
-            second[:, lanes(2 * nb + h)] = part
-            put_stats(msg, (2,), mid_blocks, 2 * nb + h, column_sum(part), column_sum(part * part))
-
-    repeat(mid // 256, second_layer)
+            second[:, lanes(4 * nb + h)] = part
+            put_stats(msg, (2,), mid_blocks, 4 * nb + h, column_sum(part), column_sum(part * part))
+
+    second_layer(none)
     sum_start(2, 0)
     merge_some(2)
     swap(0).wait_recv()
@@ -640,18 +655,18 @@
     loaded("expand")
 
     def third_layer(nb):
-        values = jnp.dot(hid_b[pl.ds(0, cells)], we[:, lanes(nb, 256)], preferred_element_type=F32)
-        third[:, lanes(nb, 256)] = values
-        for h in range(2):
+        values = jnp.dot(hid_b[pl.ds(0, cells)], we[:, lanes(nb, 512)], preferred_element_type=F32)
+        third[:, lanes(nb, 512)] = values
+        for h in range(4):
             part = values[:, h * 128 : h * 128 + 128]
             put_stats(
-                wide_msg, (0, 0), wide_blocks, 2 * nb + h, column_sum(part), column_sum(part * part)
+                wide_msg, (0, 0), wide_blocks, 4 * nb + h, column_sum(part), column_sum(part * part)
             )
 
-    repeat(wide // 256, third_layer)
+    repeat(wide // 512, third_layer)
     wide_start(0)
     merge_some(3)
-    swap(3).wait_recv()
+    swap(3).wait()
     wide_turn(0)
 
     def turn_hidden(j):
@@ -661,62 +676,67 @@
     wide_finish(0)
     center(wide_blocks)
 
-    chunk = chunk_of(image)
+    scale_c = gain_c[...] * coef[1]
+    coef[7] = scale_c
+    coef[8] = shift_c[...] - coef[0] * scale_c
 
     def normalize_c(i):
         cb = lax.rem(i + (1 - core) * (wide_blocks // 2), wide_blocks)
-        gain, shift = gain_c[pl.ds(cb, 1)], shift_c[pl.ds(cb, 1)]
         one = two = jnp.zeros((8, 128), F32)
         for k in range(n_img):
             for r in range(image // chunk):
                 at = pl.ds(k * image + r * chunk, chunk)
                 valid = mask[pl.ds(k * step + r * chunk, chunk)]
-                hat = (third[at, lanes(cb)] - row(0, cb)) * row(1, cb)
-                third[at, lanes(cb)] = hat
-                pre = hat * gain + shift + img[at, lanes(cb)].astype(F32)
-                gate = logistic(pre)
-                trunk[at, lanes(cb)] = (pre * gate * valid).astype(LOW)
-                up = merged[at, lanes(cb)] * (gate * (1.0 + pre * (1.0 - gate))) * valid
+                raw = third[at, lanes(cb)]
+                pre = raw * row(7, cb) + (row(8, cb) + img[at, lanes(cb)].astype(F32))
+                h = 0.5 * pre
+                t = jnp.tanh(h)
+                value = h + h * t
+                trunk[at, lanes(cb)] = (value * valid).astype(LOW)
+                up = merged[at, lanes(cb)] * ((1.0 + value) + t * (1.0 - value))
                 merged[at, lanes(cb)] = up
                 one = one + column_sum(up)
-                two = two + column_sum(up * hat)
+                two = two + column_sum(up * raw)
         put_stats(wide_msg, (1, 0), wide_blocks, cb, one, two)
 
-    def both_halves(body, k):
+    def both_halves(body, k, point):
         repeat(wide_blocks // 2, body)
         swap(k).start()
+        travel(point)
         repeat(wide_blocks // 2, lambda i: body(i + wide_blocks // 2))
 
-    both_halves(normalize_c, 4)
+    both_halves(normalize_c, 4, None)
     wide_start(1)
 
     swap(1).wait_recv()
     swap(4).wait_recv()
 
-    def heads_gradient(j):
-        own = trunk[:, pl.ds(pl.multiple_of(core * half + j * 256, 128), 256)]
-        both = jnp.concatenate([own, sib_two[:, lanes(j, 256)]], axis=0)
+    def heads_gradient(i):
+        own = trunk[:, pl.ds(pl.multiple_of(core * half + i * 512, 128), 512)]
+        both = jnp.concatenate([own, sib_two[:, lanes(i, 512)]], axis=0)
         values = lax.dot_general(both, hg[...], TN, preferred_element_type=F32)
-        for b in range(p.heads // 256):
-            put(HEADS, j * p.heads + b * 256, values[:, b * 256 : b * 256 + 256])
-
-    def each(family, total, body):
+        for q in range(2):
+            for b in range(p.heads // 256):
+                part = values[q * 256 : q * 256 + 256, b * 256 : b * 256 + 256]
+                put(HEADS, (2 * i + q) * p.heads + b * 256, part)
+
+    def each(family, first_part, last_part, count, body):
         n = p.parts[family]
-        per = total // n
-        for i in range(n):
-            repeat(per, lambda j, i=i: body(i * per + j))
-            travel(p.first[family] + i)
-
-    each(HEADS, half // 256, heads_gradient)
+        for i in range(first_part, last_part):
+            body(i + none)
+            for done in range(i * n // count, (i + 1) * n // count):
+                travel(p.first[family] + done)
+
+    each(HEADS, 0, half // 512, half // 512, heads_gradient)
     wide_turn(1)
 
     def head_layer(nb):
         values = jnp.dot(trunk[...], wh[:, lanes(nb, 256)], preferred_element_type=F32)
         stage[:, lanes(nb, 256)] = values.astype(LOW)
 
-    repeat(p.heads // 256, head_layer)
-    pltpu.make_async_copy(stage, head_out, out_sem.at[0]).start()
-    travel(AFTER_HEADS)
+    for i, point in enumerate((AFTER_HEADS_0, AFTER_HEADS_1, AFTER_HEADS_2)):
+        head_layer(i)
+        travel(point)
     swap(4).wait_send()
     wide_finish(1)
 
@@ -726,9 +746,14 @@
         coef[5, pl.ds(0, blocks)] = -scale * total[pl.ds(0, blocks)] / count
         coef[6, pl.ds(0, blocks)] = -scale * total[pl.ds(blocks, blocks)] / count
 
-    shift_c_grad[...] = total[pl.ds(0, wide_blocks)]
-    gain_c_grad[...] = total[pl.ds(wide_blocks, wide_blocks)]
-    backward(wide_blocks, gain_c[...], coef[1])
+    sum_up = total[pl.ds(0, wide_blocks)]
+    sum_up_hat = (total[pl.ds(wide_blocks, wide_blocks)] - coef[0] * sum_up) * coef[1]
+    shift_c_grad[...] = sum_up
+    gain_c_grad[...] = sum_up_hat
+    per_hat = -coef[7] * sum_up_hat / count
+    coef[4] = coef[7]
+    coef[5] = -coef[7] * sum_up / count - per_hat * coef[1] * coef[0]
+    coef[6] = per_hat * coef[1]
 
     def third_gradient(i):
         cb = lax.rem(i + (1 - core) * (wide_blocks // 2), wide_blocks)
@@ -739,17 +764,17 @@
                 down = merged[at, lanes(cb)] * row(4, cb) + row(5, cb) + third[at, lanes(cb)] * row(6, cb)
                 trunk[at, lanes(cb)] = (down * valid).astype(LOW)
 
-    both_halves(third_gradient, 5)
-    travel(AFTER_THIRD)
+    both_halves(third_gradient, 5, AFTER_THIRD_0)
+    travel(AFTER_THIRD_1)
 
     def slope_of(pre):
         gate = logistic(pre)
         return gate * (1.0 + pre * (1.0 - gate))
 
     def third_back(nb):
-        values = lax.dot_general(trunk[...], we[lanes(nb, 256), :], NT, preferred_element_type=F32)
-        for h in range(2):
-            cb = 2 * nb + h
+        values = lax.dot_general(trunk[...], we[lanes(nb, 512), :], NT, preferred_element_type=F32)
+        for h in range(4):
+            cb = 4 * nb + h
             one = two = jnp.zeros((8, 128), F32)
             for k in range(n_img):
                 at = pl.ds(k * image, image)
@@ -762,18 +787,20 @@
                 two = two + column_sum(up * hat)
             put_stats(msg, (3,), mid_blocks, cb, one, two)
 
-    repeat(mid // 256, third_back)
+    third_back(none)
     sum_start(3, 1)
-    travel(AFTER_BACK_B)
+    travel(AFTER_BACK_B_1)
     swap(5).wait_recv()
 
-    def expand_gradient(j):
-        own = trunk[:, pl.ds(pl.multiple_of(core * half + j * 256, 128), 256)]
-        both = jnp.concatenate([own, sib_one[:, lanes(j, 256)]], axis=0)
-        put(EXPAND, j * mid, jnp.dot(hid_b_t[...], both, preferred_element_type=F32))
-
-    each(EXPAND, half // 256, expand_gradient)
-    travel(AFTER_EXPAND)
+    def expand_gradient(i):
+        own = trunk[:, pl.ds(pl.multiple_of(core * half + i * 512, 128), 512)]
+        both = jnp.concatenate([own, sib_one[:, lanes(i, 512)]], axis=0)
+        values = jnp.dot(hid_b_t[...], both, preferred_element_type=F32)
+        for q in range(2):
+            put(EXPAND, (2 * i + q) * mid, values[:, q * 256 : q * 256 + 256])
+
+    each(EXPAND, 0, half // 512, half // 512, expand_gradient)
+    travel(AFTER_EXPAND_END)
     sum_finish(3, 1)
     shift_b_grad[...] = total[pl.ds(0, mid_blocks)]
     gain_b_grad[...] = total[pl.ds(mid_blocks, mid_blocks)]
@@ -791,6 +818,7 @@
     swap(6).start()
     own_quarter = pl.ds(pl.multiple_of(mid + core * (mid // 2), 128), mid // 2)
     low_b_all[pl.ds(0, rows)] = low_b[pl.ds(height, rows), own_quarter]
+    travel(AFTER_SECOND)
 
     def second_back(nb):
         values = None
@@ -798,13 +826,13 @@
             for j in range(3):
                 term = lax.dot_general(
                     low_b[pl.ds((2 - j) * height, rows), pl.ds((2 - i) * mid, mid)],
-                    ws[j, pl.ds(pl.multiple_of(i * mid + nb * 256, 256), 256), :],
+                    ws[j, pl.ds(pl.multiple_of(i * mid + nb * 512, 256), 512), :],
                     NT,
                     preferred_element_type=F32,
                 )
                 values = term if values is None else values + term
-        for h in range(2):
-            cb = 2 * nb + h
+        for h in range(4):
+            cb = 4 * nb + h
             one = two = jnp.zeros((8, 128), F32)
             for k in range(n_img):
                 at = pl.ds(k * image, image)
@@ -817,32 +845,19 @@
                 two = two + column_sum(up * hat)
             put_stats(msg, (4,), mid_blocks, cb, one, two)
 
-    repeat(mid // 256, second_back)
+    second_back(none)
     sum_start(4, 0)
-    travel(AFTER_BACK_A)
+    travel(AFTER_BACK_A_1)
     swap(2).wait_recv()
     swap(6).wait_recv()
-    per_tap = 3 * mid // 256
-
     def spatial_gradient(i):
-        j, k = i // per_tap, lax.rem(i, per_tap)
+        j, k = i // 2, lax.rem(i, 2)
         values = lax.dot_general(
-            hid_a[span16(j * height, p.both), lanes(k, 256)],
-            low_b_all[...],
-            TN,
-            preferred_element_type=F32,
+            hid_a[span16(j * height, p.depth), lanes(k, 768)], low_b_all[...], TN, preferred_element_type=F32
         )
-        put(SPATIAL, i * 256, values)
-
-    def spatial_some(first_part, last_part):
-        n = p.parts[SPATIAL]
-        per = 3 * per_tap // n
-        for i in range(first_part, last_part):
-            repeat(per, lambda j, i=i: spatial_gradient(i * per + j))
-            travel(p.first[SPATIAL] + i)
-
-    early = p.parts[SPATIAL] * 2 // 3
-    spatial_some(0, early)
+        put(SPATIAL, i * 768, values)
+
+    each(SPATIAL, 0, 5, 6, spatial_gradient)
     sum_finish(4, 0)
     shift_a_grad[...] = total[pl.ds(0, mid_blocks)]
     gain_a_grad[...] = total[pl.ds(mid_blocks, mid_blocks)]
@@ -859,40 +874,37 @@
     travel(AFTER_FIRST)
     swap(7).wait_recv()
 
-    def reduce_gradient(j):
-        def one(b):
-            values = jnp.dot(img_t[lanes(j, 256), :], low_a[:, lanes(b, 256)], preferred_element_type=F32)
-            put(REDUCE, j * mid + b * 256, values)
-
-        repeat(mid // 256, one)
-
-    each(REDUCE, half // 256, reduce_gradient)
-    travel(AFTER_REDUCE)
-    spatial_some(early, p.parts[SPATIAL])
-    travel(AFTER_SPATIAL)
+    def reduce_gradient(i):
+        values = jnp.dot(img_t[lanes(i, 512), :], low_a[...], preferred_element_type=F32)
+        for q in range(2):
+            for b in range(mid // 256):
+                part = values[q * 256 : q * 256 + 256, b * 256 : b * 256 + 256]
+                put(REDUCE, (2 * i + q) * mid + b * 256, part)
+
+    each(REDUCE, 0, half // 512, half // 512, reduce_gradient)
+    travel(AFTER_REDUCE_END)
+    each(SPATIAL, 5, 6, 6, spatial_gradient)
+    travel(AFTER_SPATIAL_END)
 
     def first_back(nb):
-        values = lax.dot_general(low_a[pl.ds(0, cells)], wr[lanes(nb, 256), :], NT, preferred_element_type=F32)
-        for h in range(2):
+        values = lax.dot_general(low_a[pl.ds(0, cells)], wr[lanes(nb, 512), :], NT, preferred_element_type=F32)
+        for h in range(4):
             for k in range(n_img):
                 at = pl.ds(k * image, image)
                 part = values[k * image : (k + 1) * image, h * 128 : h * 128 + 128]
-                part = (part + merged[at, lanes(2 * nb + h)]) * mask[pl.ds(k * step, image)]
-                img[at, lanes(2 * nb + h)] = part.astype(LOW)
-
-    repeat(wide // 512, first_back)
-    travel(AFTER_HALF)
-    repeat(wide // 512, lambda i: first_back(i + wide // 512))
-    pltpu.make_async_copy(img, grad_images, out_sem.at[1]).start()
+                part = (part + merged[at, lanes(4 * nb + h)]) * mask[pl.ds(k * step, image)]
+                img[at, lanes(4 * nb + h)] = part.astype(LOW)
+
+    for i, point in enumerate((AFTER_LAST_0, AFTER_LAST_1, AFTER_LAST_2, None)):
+        first_back(i + none)
+        travel(point)
 
     travel(LAST)
     for segment in p.segments:
         send, recv = beside(segment)
         take(some_of(segment, segment[2]), recv)
         take(some_of(segment, segment[2] // 2), send)
-    pltpu.make_async_copy(stage, head_out, out_sem.at[0]).wait()
-    pltpu.make_async_copy(img, grad_images, out_sem.at[1]).wait()
-    for k in (0, 1, 2, 3, 5, 6, 7):
+    for k in (0, 1, 2, 5, 6, 7):
         swap(k).wait_send()
 
 
@@ -905,7 +917,6 @@
     smem = pl.BlockSpec(memory_space=pltpu.SMEM)
     shape = jax.ShapeDtypeStruct
     scratch = [
-        pltpu.VMEM((cells, wide), LOW),
         pltpu.VMEM((wide, mid), LOW),
         pltpu.VMEM((3, 3 * mid, mid), LOW),
         pltpu.VMEM((mid, wide), LOW),
@@ -920,16 +931,14 @@
         pltpu.VMEM((cells, mid), F32),
         pltpu.VMEM((rows, mid), F32),
         pltpu.VMEM((cells, mid), F32),
-        pltpu.VMEM((p.both + 2 * p.height, 3 * mid), LOW),
+        pltpu.VMEM((p.depth + 2 * p.height, 3 * mid), LOW),
         pltpu.VMEM((2 * cells, mid), LOW),
         pltpu.VMEM((mid, 2 * cells), LOW),
         pltpu.VMEM((rows + 2 * p.height, 3 * mid), LOW),
-        pltpu.VMEM((p.both, mid // 2), LOW),
-        pltpu.VMEM((2 * cells, mid), LOW),
+        pltpu.VMEM((p.depth, mid // 2), LOW),
         pltpu.VMEM((TASKS, cells, 256), LOW),
-        pltpu.VMEM((cells, p.heads), LOW),
         pltpu.VMEM((rows, 128), F32),
-        pltpu.VMEM((7, wide_blocks, 128), F32),
+        pltpu.VMEM((9, wide_blocks, 128), F32),
         pltpu.VMEM((5, 2 * mid_blocks, 128), F32),
         pltpu.VMEM((2, p.devices, 2 * mid_blocks, 128), F32),
         pltpu.VMEM((1, 128), F32),
@@ -940,32 +949,27 @@
         pltpu.VMEM((2, p.total, 128), LOW),
         pltpu.VMEM((2, p.total, 128), LOW),
         pltpu.SemaphoreType.DMA((7,)),
-        pltpu.SemaphoreType.DMA((2,)),
         pltpu.SemaphoreType.DMA((9,)),
         pltpu.SemaphoreType.DMA((9,)),
         pltpu.SemaphoreType.DMA((8,)),
         pltpu.SemaphoreType.DMA((8,)),
         pltpu.SemaphoreType.DMA((len(p.segments), 2)),
-        pltpu.SemaphoreType.DMA((len(p.segments), 2 * p.steps + 1)),
+        pltpu.SemaphoreType.DMA((len(p.segments), p.steps + 2)),
     ]
     return pl.pallas_call(
         functools.partial(block_kernel, plan),
         out_shape=(
-            shape((cells, p.heads), LOW),
-            shape((cells, wide), LOW),
+            pltpu.VMEM((cells, p.heads), LOW),
+            pltpu.VMEM((cells, wide), LOW),
             shape((2, 2, p.total, 128), LOW),
-            shape((mid_blocks, 128), F32),
-            shape((mid_blocks, 128), F32),
-            shape((mid_blocks, 128), F32),
-            shape((mid_blocks, 128), F32),
-            shape((wide_blocks, 128), F32),
-            shape((wide_blocks, 128), F32),
+            *[pltpu.VMEM((mid_blocks, 128), F32)] * 4,
+            *[pltpu.VMEM((wide_blocks, 128), F32)] * 2,
         ),
         in_specs=[anywhere, smem] + [anywhere] * 6 + [vmem] * 6,
-        out_specs=[anywhere] * 3 + [vmem] * 6,
+        out_specs=[vmem] * 2 + [anywhere] + [vmem] * 6,
         scratch_shapes=scratch,
         compiler_params=pltpu.CompilerParams(
-            collective_id=0, has_side_effects=True, vmem_limit_bytes=63 * 2**20
+            collective_id=0, has_side_effects=True, vmem_limit_bytes=59 * 2**20
         ),
         name="block",
     )(*arrays)
@@ -977,26 +981,20 @@
     small_in = refs[3:9]
     heads_out, images_out, out_reduce, out_spatial, out_expand, out_heads = refs[9:15]
     small_out = refs[15:21]
-    low, reduce, spatial, expand, heads, heads_low, images_low, load_sem, out_sem, pass_sem = refs[21:]
-    fetches = (
-        pltpu.make_async_copy(heads_in, heads_low, pass_sem.at[0, 0]),
-        pltpu.make_async_copy(images_in, images_low, pass_sem.at[1, 0]),
+    low, reduce, spatial, expand, heads, load_sem, out_sem, pass_sem = refs[21:]
+    passes = (
+        pltpu.make_async_copy(heads_in, heads_out, pass_sem.at[0]),
+        pltpu.make_async_copy(images_in, images_out, pass_sem.at[1]),
     )
-    passes = (
-        pltpu.make_async_copy(heads_low, heads_out, pass_sem.at[0, 1]),
-        pltpu.make_async_copy(images_low, images_out, pass_sem.at[1, 1]),
-    )
-    for one in fetches:
+    for one in passes:
         one.start()
     loads = []
     for s in range(4):
         for core in range(2):
             at = (core, slice(None), pl.ds(p.base[s], p.real[s]))
-            load = pltpu.make_async_copy(gathered.at[at], low.at[at], load_sem.at[s, core])
-            load.start()
-            loads.append(load)
-    for fetch, one in zip(fetches, passes):
-        fetch.wait()
+            loads.append(pltpu.make_async_copy(gathered.at[at], low.at[at], load_sem.at[s, core]))
+    ahead = 3
+    for one in loads[:ahead]:
         one.start()
     for src, dst in zip(small_in, small_out):
         dst[...] = src[...]
@@ -1011,6 +1009,8 @@
     for s, (wide, out, height, width, by_rows) in enumerate(where):
         for core in range(2):
             loads[2 * s + core].wait()
+            for one in loads[2 * s + core + ahead :][:1]:
+                one.start()
             size = 256
             row_at = core * height if by_rows else 0
             col_at = 0 if by_rows else core * width
@@ -1053,20 +1053,21 @@
             *(shape(one, F32) for one in full),
             *(shape(one.shape, F32) for one in small),
         ),
-        in_specs=[anywhere] * 3 + [vmem] * 6,
+        in_specs=[anywhere] + [vmem] * 8,
         out_specs=[anywhere] * 6 + [vmem] * 6,
         scratch_shapes=[
             pltpu.VMEM(gathered.shape, LOW),
             *(pltpu.VMEM(one, F32) for one in full),
-            pltpu.VMEM(head_out.shape, LOW),
-            pltpu.VMEM(grad_images.shape, LOW),
             pltpu.SemaphoreType.DMA((4, 2)),
             pltpu.SemaphoreType.DMA((4, 2)),
-            pltpu.SemaphoreType.DMA((2, 2)),
+            pltpu.SemaphoreType.DMA((2,)),
         ],
-        compiler_params=pltpu.CompilerParams(vmem_limit_bytes=56 * 2**20),
+        compiler_params=pltpu.CompilerParams(vmem_limit_bytes=48 * 2**20),
         name="widen",
-    )(gathered, head_out, grad_images, *small)
+    )(
+        gathered,
+        *(pltpu.with_memory_space_constraint(one, pltpu.VMEM) for one in (head_out, grad_images, *small)),
+    )
 
 
 def solution(mesh):

time: 160 us -> 154 us (0.963)
  Pallas kernels: 159 us -> 153 us
    pallas_call x1, Pallas kernels: 143 us -> 139 us  [run_block(): pl.pallas_call(functools.partial(block_kernel, plan), out_shape=(pltpu.VM...]
    pallas_call x1, Pallas kernels: 15.8 us -> 13.5 us  [widen(): pl.pallas_call(functools.partial(widen_kernel, plan), out_shape=(shape(he...]
where the time goes in v3:
time: 154 us
  Pallas kernels  153 us (99%)
    pallas_call x1, Pallas kernels, run_block(): pl.pallas_call(functools.partial(block_kernel, plan), out_shape=(pltpu.VM...  139 us
    pallas_call x1, Pallas kernels, widen(): pl.pallas_call(functools.partial(widen_kernel, plan), out_shape=(shape(he...  13.5 us

profile of v3, /device:TPU:0, one launch (start us, length us, event | category | flops | bytes accessed | tf_op | source)
XLA Modules:
  0.0 153.6 jit_solution(15308589863271636905)
XLA Ops:
  0.6 139.2 %block.1 = (bf16[576,768]{1,0:T(8,128)(2,1)S(1)}, bf16[576,2048]{1,0:T(8,128)(2,1)S(1)}, bf16[2,2,11776,128]{3,2,1,0:T(8,128)(2,1)}, f32[4,128]{1,0:T(4,128)S(1)...) custom-call(bf16[576,2048]{1,0:T(8,128)(2,1)} %bitcast.30, ...), custom_call_target="tpu_custom_call" | custom-call | tf_op jit(solution)/shard_map/block/pallas_call | solution.py:959
  139.9 13.5 %widen.1 = (bf16[576,768]{1,0:T(8,128)(2,1)}, bf16[576,2048]{1,0:T(8,128)(2,1)}, f32[2048,512]{1,0:T(8,128)}, f32[4608,512]{1,0:T(8,128)}, f32[512,2048]{1,0:T(8...) custom-call(bf16[2,2,11776,128]{3,2,1,0:T(8,128)(2,1)} %get-tuple-el, ...), custom_call_target="tpu_custom_call" | custom-call | tf_op jit(solution)/shard_map/widen/pallas_call | solution.py:1048

commit v4 on v3

--- a/solution.py
+++ b/solution.py
@@ -175,6 +175,8 @@
     head_out,
     grad_images,
     gathered,
+    terms,
+    received,
     gain_a_grad,
     shift_a_grad,
     gain_b_grad,
@@ -213,8 +215,6 @@
         wide_msg,
         wide_slots,
         total,
-        terms,
-        received,
         load_sem,
         sum_send,
         sum_recv,
@@ -465,14 +465,29 @@
             if k == 0:
                 remote(ours, ours, *beside(segment), sibling).start()
 
+    shared = []
+
     def share(segment):
-        _, at, size, kind = segment
+        index, at, size, kind = segment
         settle(segment, p.steps, size // 2, size // 2)
-        take(some_of(segment, size // 2), ring_send.at[segment[0], 1])
+        take(some_of(segment, size // 2), ring_send.at[index, 1])
         for part in range(2):
             bit = route(kind, part)[0][0]
             ours = home(part, at + (1 - bit) * (size // 2), size // 2)
             remote(ours, ours, *beside(segment), sibling).start()
+        rows_here = pl.ds(at, size)
+        pltpu.make_async_copy(gathered.at[core, :, rows_here], received.at[:, rows_here], ring_send.at[index, 0]).start()
+        for other in shared[-1:]:
+            bring(other)
+        shared.append(segment)
+
+    def bring(segment):
+        index, at, size, _ = segment
+        send, recv = beside(segment)
+        take(some_of(segment, size), recv)
+        take(some_of(segment, size // 2), send)
+        rows_here = pl.ds(at, size)
+        pltpu.make_async_copy(gathered.at[1 - core, :, rows_here], terms.at[:, rows_here], ring_send.at[index, 0]).start()
 
     def travel(point):
         for todo in p.agenda.get(point, ()):
@@ -900,10 +915,9 @@
         travel(point)
 
     travel(LAST)
-    for segment in p.segments:
-        send, recv = beside(segment)
-        take(some_of(segment, segment[2]), recv)
-        take(some_of(segment, segment[2] // 2), send)
+    bring(shared[-1])
+    for index, at, size, _ in p.segments:
+        take(gathered.at[:, :, pl.ds(at, size)], ring_send.at[index, 0])
     for k in (0, 1, 2, 5, 6, 7):
         swap(k).wait_send()
 
@@ -946,8 +960,6 @@
         pltpu.VMEM((2, 2, 2 * wide_blocks, 128), F32),
         pltpu.VMEM((2, 2 * p.tasks + p.line, 2 * wide_blocks, 128), F32),
         pltpu.VMEM((2 * wide_blocks, 128), F32),
-        pltpu.VMEM((2, p.total, 128), LOW),
-        pltpu.VMEM((2, p.total, 128), LOW),
         pltpu.SemaphoreType.DMA((7,)),
         pltpu.SemaphoreType.DMA((9,)),
         pltpu.SemaphoreType.DMA((9,)),
@@ -962,14 +974,15 @@
             pltpu.VMEM((cells, p.heads), LOW),
             pltpu.VMEM((cells, wide), LOW),
             shape((2, 2, p.total, 128), LOW),
+            *[pltpu.VMEM((2, p.total, 128), LOW)] * 2,
             *[pltpu.VMEM((mid_blocks, 128), F32)] * 4,
             *[pltpu.VMEM((wide_blocks, 128), F32)] * 2,
         ),
         in_specs=[anywhere, smem] + [anywhere] * 6 + [vmem] * 6,
-        out_specs=[vmem] * 2 + [anywhere] + [vmem] * 6,
+        out_specs=[vmem] * 2 + [anywhere] + [vmem] * 8,
         scratch_shapes=scratch,
         compiler_params=pltpu.CompilerParams(
-            collective_id=0, has_side_effects=True, vmem_limit_bytes=59 * 2**20
+            collective_id=0, has_side_effects=True, vmem_limit_bytes=47 * 2**20
         ),
         name="block",
     )(*arrays)
@@ -977,25 +990,15 @@
 
 def widen_kernel(plan, *refs):
     p = plan
-    gathered, heads_in, images_in = refs[:3]
-    small_in = refs[3:9]
-    heads_out, images_out, out_reduce, out_spatial, out_expand, out_heads = refs[9:15]
-    small_out = refs[15:21]
-    low, reduce, spatial, expand, heads, load_sem, out_sem, pass_sem = refs[21:]
+    other, own, heads_in, images_in = refs[:4]
+    small_in = refs[4:10]
+    heads_out, images_out, out_reduce, out_spatial, out_expand, out_heads = refs[10:16]
+    small_out = refs[16:22]
+    reduce, spatial, expand, heads, out_sem, pass_sem = refs[22:]
     passes = (
         pltpu.make_async_copy(heads_in, heads_out, pass_sem.at[0]),
         pltpu.make_async_copy(images_in, images_out, pass_sem.at[1]),
     )
-    for one in passes:
-        one.start()
-    loads = []
-    for s in range(4):
-        for core in range(2):
-            at = (core, slice(None), pl.ds(p.base[s], p.real[s]))
-            loads.append(pltpu.make_async_copy(gathered.at[at], low.at[at], load_sem.at[s, core]))
-    ahead = 3
-    for one in loads[:ahead]:
-        one.start()
     for src, dst in zip(small_in, small_out):
         dst[...] = src[...]
     where = (
@@ -1006,16 +1009,15 @@
     )
     copies = []
     per_tap = p.mid // 256
+    size = 256
+    mine = lax.rem(lax.axis_index("dp"), 2)
     for s, (wide, out, height, width, by_rows) in enumerate(where):
-        for core in range(2):
-            loads[2 * s + core].wait()
-            for one in loads[2 * s + core + ahead :][:1]:
-                one.start()
-            size = 256
+        for low, core in ((own, mine), (other, 1 - mine)):
             row_at = core * height if by_rows else 0
             col_at = 0 if by_rows else core * width
-
-            def one(i, s=s, wide=wide, out=out, row_at=row_at, col_at=col_at, core=core):
+            sem = out_sem.at[s, core]
+
+            def one(i, s=s, wide=wide, out=out, low=low, row_at=row_at, col_at=col_at, sem=sem):
                 rows = pl.ds(pl.multiple_of(row_at + i * size, size), size)
                 for b in range(width // 256):
                     if s == EXPAND:
@@ -1027,24 +1029,27 @@
                         start = i * width + b * size
                     src = pl.ds(pl.multiple_of(p.base[s] + start, size), size)
                     for part in range(2):
-                        cols = pl.ds(col_at + b * 256 + part * 128, 128)
-                        wide[rows, cols] = low[core, part, src, :].astype(F32)
-                at = (rows, pl.ds(col_at, width))
-                pltpu.make_async_copy(wide.at[at], out.at[at], out_sem.at[s, core]).start()
+                        cols = pl.ds(pl.multiple_of(col_at + b * 256 + part * 128, 128), 128)
+                        wide[rows, cols] = low[part, src, :].astype(F32)
+                at = (rows, pl.ds(pl.multiple_of(col_at, 128), width))
+                pltpu.make_async_copy(wide.at[at], out.at[at], sem).start()
 
             repeat(height // size, one)
-            at = (pl.ds(row_at, height), pl.ds(col_at, width))
-            copies.append(pltpu.make_async_copy(wide.at[at], out.at[at], out_sem.at[s, core]))
+            at = (pl.ds(pl.multiple_of(row_at, size), height), pl.ds(pl.multiple_of(col_at, 128), width))
+            copies.append(pltpu.make_async_copy(wide.at[at], out.at[at], sem))
+    for one in passes:
+        one.start()
     for one in copies + list(passes):
         one.wait()
 
 
-def widen(plan, head_out, grad_images, gathered, *small):
+def widen(plan, head_out, grad_images, _, terms, received, *small):
     p = plan
     anywhere = pl.BlockSpec(memory_space=pl.ANY)
     vmem = pl.BlockSpec(memory_space=pltpu.VMEM)
     shape = jax.ShapeDtypeStruct
     full = ((p.wide, p.mid), (9 * p.mid, p.mid), (p.mid, p.wide), (p.wide, p.heads))
+    held = (terms, received, head_out, grad_images, *small)
     return pl.pallas_call(
         functools.partial(widen_kernel, plan),
         out_shape=(
@@ -1053,21 +1058,16 @@
             *(shape(one, F32) for one in full),
             *(shape(one.shape, F32) for one in small),
         ),
-        in_specs=[anywhere] + [vmem] * 8,
+        in_specs=[vmem] * 10,
         out_specs=[anywhere] * 6 + [vmem] * 6,
         scratch_shapes=[
-            pltpu.VMEM(gathered.shape, LOW),
             *(pltpu.VMEM(one, F32) for one in full),
-            pltpu.SemaphoreType.DMA((4, 2)),
             pltpu.SemaphoreType.DMA((4, 2)),
             pltpu.SemaphoreType.DMA((2,)),
         ],
-        compiler_params=pltpu.CompilerParams(vmem_limit_bytes=48 * 2**20),
+        compiler_params=pltpu.CompilerParams(vmem_limit_bytes=32 * 2**20),
         name="widen",
-    )(
-        gathered,
-        *(pltpu.with_memory_space_constraint(one, pltpu.VMEM) for one in (head_out, grad_images, *small)),
-    )
+    )(*(pltpu.with_memory_space_constraint(one, pltpu.VMEM) for one in held))
 
 
 def solution(mesh):

time: 154 us -> 151 us (0.981)
  Pallas kernels: 153 us -> 150 us
    pallas_call x1, Pallas kernels: 13.5 us -> 9.77 us  [widen(): pl.pallas_call(functools.partial(widen_kernel, plan), out_shape=(shape(he...]
where the time goes in v4:
time: 151 us
  Pallas kernels  150 us (99%)
    pallas_call x1, Pallas kernels, run_block(): pl.pallas_call(functools.partial(block_kernel, plan), out_shape=(pltpu.VM...  141 us
    pallas_call x1, Pallas kernels, widen(): pl.pallas_call(functools.partial(widen_kernel, plan), out_shape=(shape(he...  9.77 us

profile of v4, /device:TPU:0, one launch (start us, length us, event | category | flops | bytes accessed | tf_op | source)
XLA Modules:
  0.0 151.3 jit_solution(12956785644747243719)
XLA Ops:
  0.6 140.7 %block.1 = (bf16[576,768]{1,0:T(8,128)(2,1)S(1)}, bf16[576,2048]{1,0:T(8,128)(2,1)S(1)}, bf16[2,2,11776,128]{3,2,1,0:T(8,128)(2,1)}, bf16[2,11776,128]{2,1,0:T(8...) custom-call(bf16[576,2048]{1,0:T(8,128)(2,1)} %bitcast.30, ...), custom_call_target="tpu_custom_call" | custom-call | tf_op jit(solution)/shard_map/block/pallas_call | solution.py:971
  141.3 9.8 %widen.1 = (bf16[576,768]{1,0:T(8,128)(2,1)}, bf16[576,2048]{1,0:T(8,128)(2,1)}, f32[2048,512]{1,0:T(8,128)}, f32[4608,512]{1,0:T(8,128)}, f32[512,2048]{1,0:T(8...) custom-call(bf16[2,11776,128]{2,1,0:T(8,128)(2,1)S(1)} %get-tuple-el, ...), custom_call_target="tpu_custom_call" | custom-call | tf_op jit(solution)/shard_map/widen/pallas_call | solution.py:1053

commit v5 on v4

--- a/solution.py
+++ b/solution.py
@@ -17,7 +17,7 @@
 TN = (((0,), (0,)), ((), ()))
 HEADS, EXPAND, SPATIAL, REDUCE = range(4)
 PARTS = (4, 2, 6, 4)
-ROUTES = (0, 0, 0, 0, 5, 0, 5, 0, 0, 0, 0, 3, 5, 4, 0, 3)
+ROUTES = (0, 0, 0, 0, 5, 0, 5, 0, 0, 0, 0, 4, 5, 0, 0, 3)
 (
     AFTER_HEADS_0,
     AFTER_HEADS_1,
@@ -27,6 +27,8 @@
     AFTER_BACK_B_1,
     AFTER_EXPAND_END,
     AFTER_SECOND,
+    AFTER_TAP_0,
+    AFTER_TAP_1,
     AFTER_BACK_A_1,
     AFTER_FIRST,
     AFTER_REDUCE_END,
@@ -35,7 +37,7 @@
     AFTER_LAST_1,
     AFTER_LAST_2,
     LAST,
-) = range(100, 116)
+) = range(100, 118)
 AGENDA = {
     0: (0,),
     1: (10,),
@@ -46,26 +48,27 @@
     4: (40,),
     5: (50, 31,),
     AFTER_EXPAND_END: (2, 12,),
-    AFTER_BACK_A_1: (22, 51, 32,),
+    AFTER_TAP_0: (22,),
+    AFTER_BACK_A_1: (51, 32,),
     6: (60, 41,),
     7: (70, 3, 13,),
-    8: (80,),
-    9: (90, 23, 52,),
-    10: (100, 33, 42,),
+    8: (80, 23,),
+    9: (90, 52, 33,),
+    10: (100, 42,),
+    11: (110,),
     12: (120, 71,),
-    13: (130,),
-    14: (140, 61,),
-    15: (150, 4, 81,),
-    11: (110, 24, 14,),
-    AFTER_LAST_0: (91, 53,),
-    AFTER_LAST_1: (34,),
+    13: (130, 61, 4,),
+    14: (140, 14,),
+    15: (150, 81, 24,),
+    AFTER_REDUCE_END: (53,),
+    AFTER_LAST_0: (91, 34,),
     AFTER_LAST_2: (101,),
     LAST: (
-        72, 43, 121, 141, 131, 62, 5, 25, 151, 15, 54, 82, 35, 73, 111, 44, 6, 92, 26, 102, 122, 152, 142, 16,
-        132, 63, 55, 7, 83, 27, 36, 123, 153, 74, 17, 112, 8, 45, 93, 103, 28, 143, 37, 133, 64, 56, 18, 113,
-        84, 124, 46, 154, 75, 94, 104, 38, 134, 144, 65, 114, 57, 85, 76, 135, 47, 125, 155, 66, 95, 105, 86, 145,
-        58, 115, 77, 126, 156, 136, 67, 87, 116, 48, 96, 78, 127, 106, 137, 146, 157, 88, 97, 107, 147, 68, 158, 117,
-        98, 108, 128, 148, 138, 118,
+        72, 43, 111, 131, 62, 121, 141, 5, 15, 25, 151, 54, 35, 82, 73, 92, 44, 102, 6, 112, 16, 132, 26, 63,
+        122, 152, 142, 7, 55, 36, 17, 83, 27, 123, 74, 153, 93, 45, 8, 103, 37, 113, 133, 64, 143, 18, 56, 28,
+        84, 124, 46, 75, 154, 94, 104, 38, 134, 114, 65, 144, 85, 57, 125, 76, 47, 155, 115, 66, 95, 105, 86, 135,
+        145, 58, 126, 77, 156, 67, 87, 48, 127, 116, 96, 78, 106, 136, 146, 88, 117, 157, 97, 107, 137, 147, 68, 158,
+        98, 128, 108, 138, 118, 148,
     ),
 }
 
@@ -261,8 +264,10 @@
         )
 
     loads = {
-        "images": (images, img),
-        "reduce": (w_reduce, wr),
+        "i0": (images.at[:, pl.ds(0, half)], img.at[:, pl.ds(0, half)]),
+        "w0": (w_reduce.at[pl.ds(0, half)], wr.at[pl.ds(0, half)]),
+        "i1": (images.at[:, pl.ds(half, half)], img.at[:, pl.ds(half, half)]),
+        "w1": (w_reduce.at[pl.ds(half, half)], wr.at[pl.ds(half, half)]),
         "grad": (head_grad, hg.at[pl.ds(0, cells)]),
         "heads": (w_heads, wh),
         "limits": (limits, trunk),
@@ -273,10 +278,10 @@
     def load(key):
         pltpu.make_async_copy(*loads[key], load_sem.at[order.index(key)]).start()
 
-    load("images")
-    load("reduce")
+    for key in order[:4]:
+        load(key)
     repeat(p.devices - 1, greet)
-    for key in order[2:]:
+    for key in order[4:]:
         load(key)
     for row_tap in range(3):
         for col_tap in range(3):
@@ -522,11 +527,15 @@
 
     count_msg[...] = fold(column_sum(mask[...]))
     count_slots[me] = count_msg[...]
-    loaded("images")
-    loaded("reduce")
+    loaded("i0")
+    loaded("w0")
 
     def first_layer(nb):
-        values = jnp.dot(img[...], wr[:, lanes(nb, 512)], preferred_element_type=F32)
+        front, rear = pl.ds(0, half), pl.ds(half, half)
+        values = jnp.dot(img[:, front], wr[front, lanes(nb, 512)], preferred_element_type=F32)
+        loaded("i1")
+        loaded("w1")
+        values = values + jnp.dot(img[:, rear], wr[rear, lanes(nb, 512)], preferred_element_type=F32)
         for h in range(4):
             one = two = jnp.zeros((8, 128), F32)
             for k in range(n_img):
@@ -573,7 +582,7 @@
         repeat(cells // chunk, drop)
 
     blocks = wide // 256
-    cuts = [0, blocks // 4, blocks * 5 // 8, blocks * 6 // 8, blocks]
+    cuts = [0, blocks // 8, blocks * 5 // 8, blocks * 6 // 8, blocks]
 
     def merge_some(k):
         lax.fori_loop(cuts[k], cuts[k + 1], lambda i, carry: (merge(i), carry)[1], 0)
@@ -846,6 +855,7 @@
                     preferred_element_type=F32,
                 )
                 values = term if values is None else values + term
+            travel((AFTER_TAP_0, AFTER_TAP_1, None)[i])
         for h in range(4):
             cb = 4 * nb + h
             one = two = jnp.zeros((8, 128), F32)
@@ -872,7 +882,7 @@
         )
         put(SPATIAL, i * 768, values)
 
-    each(SPATIAL, 0, 5, 6, spatial_gradient)
+    each(SPATIAL, 0, 6, 6, spatial_gradient)
     sum_finish(4, 0)
     shift_a_grad[...] = total[pl.ds(0, mid_blocks)]
     gain_a_grad[...] = total[pl.ds(mid_blocks, mid_blocks)]
@@ -898,7 +908,7 @@
 
     each(REDUCE, 0, half // 512, half // 512, reduce_gradient)
     travel(AFTER_REDUCE_END)
-    each(SPATIAL, 5, 6, 6, spatial_gradient)
+    each(SPATIAL, 6, 6, 6, spatial_gradient)
     travel(AFTER_SPATIAL_END)
 
     def first_back(nb):
@@ -960,7 +970,7 @@
         pltpu.VMEM((2, 2, 2 * wide_blocks, 128), F32),
         pltpu.VMEM((2, 2 * p.tasks + p.line, 2 * wide_blocks, 128), F32),
         pltpu.VMEM((2 * wide_blocks, 128), F32),
-        pltpu.SemaphoreType.DMA((7,)),
+        pltpu.SemaphoreType.DMA((9,)),
         pltpu.SemaphoreType.DMA((9,)),
         pltpu.SemaphoreType.DMA((9,)),
         pltpu.SemaphoreType.DMA((8,)),
@@ -982,7 +992,7 @@
         out_specs=[vmem] * 2 + [anywhere] + [vmem] * 8,
         scratch_shapes=scratch,
         compiler_params=pltpu.CompilerParams(
-            collective_id=0, has_side_effects=True, vmem_limit_bytes=47 * 2**20
+            collective_id=0, has_side_effects=True, vmem_limit_bytes=95 * 2**19
         ),
         name="block",
     )(*arrays)
@@ -999,6 +1009,8 @@
         pltpu.make_async_copy(heads_in, heads_out, pass_sem.at[0]),
         pltpu.make_async_copy(images_in, images_out, pass_sem.at[1]),
     )
+    for one in passes:
+        one.start()
     for src, dst in zip(small_in, small_out):
         dst[...] = src[...]
     where = (
@@ -1037,8 +1049,6 @@
             repeat(height // size, one)
             at = (pl.ds(pl.multiple_of(row_at, size), height), pl.ds(pl.multiple_of(col_at, 128), width))
             copies.append(pltpu.make_async_copy(wide.at[at], out.at[at], sem))
-    for one in passes:
-        one.start()
     for one in copies + list(passes):
         one.wait()
 

time: 151 us -> 151 us (level)
  no operation moved by 1% of the time
where the time goes in v5:
time: 151 us
  Pallas kernels  150 us (99%)
    pallas_call x1, Pallas kernels, run_block(): pl.pallas_call(functools.partial(block_kernel, plan), out_shape=(pltpu.VM...  140 us
    pallas_call x1, Pallas kernels, widen(): pl.pallas_call(functools.partial(widen_kernel, plan), out_shape=(shape(he...  9.71 us

profile of v5, /device:TPU:0, one launch (start us, length us, event | category | flops | bytes accessed | tf_op | source)
XLA Modules:
  0.0 150.7 jit_solution(1945437864937205747)
XLA Ops:
  0.6 140.1 %block.1 = (bf16[576,768]{1,0:T(8,128)(2,1)S(1)}, bf16[576,2048]{1,0:T(8,128)(2,1)S(1)}, bf16[2,2,11776,128]{3,2,1,0:T(8,128)(2,1)}, bf16[2,11776,128]{2,1,0:T(8...) custom-call(bf16[576,2048]{1,0:T(8,128)(2,1)} %bitcast.30, ...), custom_call_target="tpu_custom_call" | custom-call | tf_op jit(solution)/shard_map/block/pallas_call | solution.py:981
  140.8 9.7 %widen.1 = (bf16[576,768]{1,0:T(8,128)(2,1)}, bf16[576,2048]{1,0:T(8,128)(2,1)}, f32[2048,512]{1,0:T(8,128)}, f32[4608,512]{1,0:T(8,128)}, f32[512,2048]{1,0:T(8...) custom-call(bf16[2,11776,128]{2,1,0:T(8,128)(2,1)S(1)} %get-tuple-el, ...), custom_call_target="tpu_custom_call" | custom-call | tf_op jit(solution)/shard_map/widen/pallas_call | solution.py:1063
